TPU v7x, 128 devices: a whole 4x4x4 slice. The times are simulated.
128 devices in a mesh: inst: 4 (over z), seq: 32 (over y, x, core).
Axes of the slice: x: 4, y: 4, z: 4, core: 2. Of those that a mesh axis runs over, the one named last changes fastest.
Arguments:
- kv_pool: bfloat16 [4096, 128, 2048], P(('inst', 'seq')), may hold values from -6 to 6
- queries: bfloat16 [2, 32, 8192], P(None, 'inst', 'seq'), may hold values from -260 to 260
- new_kv: bfloat16 [2, 32, 2048], P(None, 'inst', 'seq'), may hold values from -6 to 6
- lengths: int32 [32], replicated, may hold values from 4097 to 16384, as said below
- block_dev: int32 [32, 128], replicated, may hold values from -1 to 127, as said below
- block_slot: int32 [32, 128], replicated, may hold values from -1 to 31, as said below
- owner_dev: int32 [2, 32], replicated, may hold values from 0 to 127, as said below
- owner_row: int32 [2, 32], replicated, may hold values from 0 to 3, as said below
Outputs:
- attn_out: bfloat16 [2, 32, 8192], P(None, 'inst', 'seq')
- tail_kv: bfloat16 [512, 2048], P(('inst', 'seq'))
Inputs may be any that keep to these rules, and one draw needn't show every extreme that they name: `lengths`: in each index of inst one request of the instance has exactly 16384 tokens. `block_dev`: entries b < ceil(lengths[r] / 128) name distinct (device, slot) pairs with block_slot, on any device of the slice; all later entries are -1 in both tables. `block_slot`: see block_dev. No two new rows share a pair (owner_dev, owner_row). `owner_row`: see owner_dev.
All inputs are finite; a program needn't handle non-finite values.
Results may differ from a plain program's by a relative error of at most 0.0027.
Values may be sent and summed in bfloat16 or wider, within the bound.
A program may use at most 128 MiB of HBM per device.

v0:
```python
import math

import jax
import jax.numpy as jnp
from jax import lax
from jax.sharding import PartitionSpec as P

H = 64
KVH = 8
HD = 128
TAIL = 4


masked_low = -1e30


def group_terms(scores, valid_mask):
    masked = jnp.where(valid_mask, scores, masked_low)
    peak_value = jnp.max(masked, axis=-1)
    weights = jnp.where(valid_mask, jnp.exp(masked - peak_value[..., None]), 0.0).astype(
        jnp.bfloat16
    )
    totals = jnp.sum(weights.astype(jnp.float32), axis=-1)
    return (peak_value, weights, totals)


def rescaled(peak_dev, den_dev, num_dev):
    peak_all = lax.pmax(peak_dev, ("inst", "seq"))
    factor = jnp.exp(peak_dev - peak_all)
    return (den_dev * factor, num_dev * factor[..., None])


def per_device(kv_pool, queries, new_kv, lengths, block_dev, block_slot, owner_dev, owner_row):
    seq_count = lax.axis_size("seq")
    inst_count = lax.axis_size("inst")
    my_device = lax.axis_index("inst") * seq_count + lax.axis_index("seq")
    wide_parts = (
        lax.all_gather(queries, "seq", axis=2, tiled=True),
        lax.all_gather(new_kv, "seq", axis=2, tiled=True),
    )
    q_all, new_rows = (
        lax.all_gather(wide_parts[0], "inst", axis=1, tiled=True),
        lax.all_gather(wide_parts[1], "inst", axis=1, tiled=True),
    )
    step_count = q_all.shape[0]
    req_total = q_all.shape[1]
    req_local = queries.shape[1]
    groups = H // KVH
    head_scale = 1.0 / math.sqrt(HD)
    q_heads = q_all.reshape(step_count, req_total, KVH, groups, HD)
    slot_count = kv_pool.shape[0]
    block_len = kv_pool.shape[1]
    key_rows = kv_pool[:, :, : KVH * HD].reshape(slot_count, block_len, KVH, HD)
    value_rows = kv_pool[:, :, KVH * HD :].reshape(slot_count, block_len, KVH, HD)
    table_width = block_dev.shape[1]
    entry_ids = jnp.arange(req_total * table_width, dtype=jnp.int32)
    slot_ids = jnp.arange(slot_count, dtype=jnp.int32)
    hit_mask = (block_dev.reshape(-1)[:, None] == my_device) & (
        block_slot.reshape(-1)[:, None] == slot_ids[None, :]
    )
    hit_count = hit_mask.astype(jnp.int32)
    slot_req = jnp.sum(hit_count * (entry_ids // table_width)[:, None], axis=0)
    slot_blk = jnp.sum(hit_count * (entry_ids % table_width)[:, None], axis=0)
    used_mask = jnp.any(hit_mask, axis=0)
    slot_len = jnp.take(lengths, slot_req)
    position = slot_blk[:, None] * block_len + jnp.arange(block_len, dtype=jnp.int32)[None, :]
    valid_mask = used_mask[:, None] & (position < slot_len[:, None])
    q_slot = jnp.take(q_heads, slot_req, axis=1)
    scores = (
        jnp.einsum("sngqd,ntgd->sngqt", q_slot, key_rows, preferred_element_type=jnp.float32)
        * head_scale
    )
    peak_slot, weights, totals_slot = group_terms(scores, valid_mask[None, :, None, None, :])
    num_slot = jnp.einsum(
        "sngqt,ntgd->sngqd", weights, value_rows, preferred_element_type=jnp.float32
    )
    row_parts = new_rows.reshape(step_count, req_total, 2, KVH, HD)
    step_order = jnp.arange(step_count, dtype=jnp.int32)
    reach_mask = step_order[None, :] <= step_order[:, None]
    scores_new = (
        jnp.einsum(
            "srgqd,jrgd->srgqj", q_heads, row_parts[:, :, 0], preferred_element_type=jnp.float32
        )
        * head_scale
    )
    peak_new, weights_new, totals_new = group_terms(scores_new, reach_mask[:, None, None, None, :])
    num_new = jnp.einsum(
        "srgqj,jrgd->srgqd", weights_new, row_parts[:, :, 1], preferred_element_type=jnp.float32
    )
    owned_mask = (owner_dev == my_device)[:, :, None, None]
    member = (slot_req[None, :] == jnp.arange(req_total, dtype=jnp.int32)[:, None]) & used_mask[
        None, :
    ]
    peak_cache = jnp.max(
        jnp.where(member[None, :, :, None, None], peak_slot[:, None], masked_low), axis=2
    )
    peak_dev = jnp.maximum(peak_cache, jnp.where(owned_mask, peak_new, masked_low))
    factor_slot = jnp.exp(peak_slot - jnp.take(peak_dev, slot_req, axis=1))
    member_float = member.astype(jnp.float32)
    highest = lax.Precision.HIGHEST
    num_dev = jnp.einsum(
        "rn,sngqd->srgqd", member_float, num_slot * factor_slot[..., None], precision=highest
    )
    den_dev = jnp.einsum(
        "rn,sngq->srgq", member_float, totals_slot * factor_slot, precision=highest
    )
    factor_new = jnp.where(owned_mask, jnp.exp(peak_new - peak_dev), 0.0)
    num_dev = num_dev + num_new * factor_new[..., None]
    den_dev = den_dev + totals_new * factor_new
    heads_dev = H // seq_count
    width_dev = heads_dev * HD
    den_term, num_term = rescaled(peak_dev, den_dev, num_dev)
    num_term = num_term.reshape(step_count, inst_count, req_local, seq_count, width_dev)
    den_term = den_term.reshape(step_count, inst_count, req_local, seq_count, heads_dev)
    num_flat = jnp.transpose(num_term, (1, 3, 0, 2, 4)).reshape(
        inst_count * seq_count, step_count, req_local, width_dev
    )
    den_flat = jnp.transpose(den_term, (1, 3, 0, 2, 4)).reshape(
        inst_count * seq_count, step_count, req_local, heads_dev
    )
    num_part, den_part = (
        lax.psum_scatter(num_flat, ("inst", "seq"), scatter_dimension=0, tiled=True),
        lax.psum_scatter(den_flat, ("inst", "seq"), scatter_dimension=0, tiled=True),
    )
    num_mine = num_part.reshape(step_count, req_local, heads_dev, HD)
    den_mine = den_part.reshape(step_count, req_local, heads_dev)
    result = (
        (num_mine / den_mine[..., None])
        .astype(jnp.bfloat16)
        .reshape(step_count, req_local, width_dev)
    )
    flat_rows = new_rows.reshape(step_count * req_total, 2 * KVH * HD)
    pick_mask = (owner_dev.reshape(-1)[None, :] == my_device) & (
        owner_row.reshape(-1)[None, :] == jnp.arange(TAIL, dtype=jnp.int32)[:, None]
    )
    tail_rows = jnp.dot(
        pick_mask.astype(jnp.bfloat16), flat_rows, preferred_element_type=jnp.float32
    ).astype(jnp.bfloat16)
    return (result, tail_rows)


def solution(mesh):
    placed = (
        P(("inst", "seq"), None, None),
        P(None, "inst", "seq"),
        P(None, "inst", "seq"),
        P(),
        P(),
        P(),
        P(),
        P(),
    )
    return jax.shard_map(
        per_device,
        mesh=mesh,
        in_specs=placed,
        out_specs=(P(None, "inst", "seq"), P(("inst", "seq"), None)),
        check_vma=False,
    )
```

profile of v0, /device:TPU:1, one launch (start us, length us, event | category | flops | bytes accessed | tf_op | source)
XLA Modules:
  0.0 865.7 jit_solution(3476255955965798573)
XLA Ops:
  7.2 29.0 %all_gather.12 = bf16[2,8,8192]{2,1,0:T(8,128)(2,1)} all-gather(bf16[2,8,256]{2,1,0:T(8,128)(2,1)} %param.9), channel_id=1, replica_groups=mesh['inst'=4,'seq'=32] {'seq'}, dimensions={2}, use_global_device_ids=true | all-gather | bytes 270336 | tf_op jit(solution)/shard_map/all_gather | solution.py:38
  38.0 12.1 %fusion.39 = (bf16[32,128,1024]{2,1,0:T(8,128)(2,1)}, bf16[32,128,1024]{2,1,0:T(8,128)(2,1)}) fusion(bf16[32,128,2048]{2,1,0:T(8,128)(2,1)} %param.8), kind=kLoop, calls=%fused_computation.77 | loop fusion | bytes 33554432 | tf_op jit(solution)/shard_map/slice | solution.py:53
  50.1 11.9 %copy.179 = bf16[32,128,1024]{1,2,0:T(8,128)(2,1)} copy(bf16[32,128,1024]{2,1,0:T(8,128)(2,1)} %get-tuple-element.10) | data formatting | bytes 16777216
  62.1 23.9 %all_gather.14 = bf16[2,8,2048]{1,0,2:T(2,128)(2,1)S(1)} all-gather(bf16[2,8,64]{1,0,2:T(2,128)(2,1)S(1)} %copy.147), channel_id=1, replica_groups=mesh['inst'=4,'seq'=32] {'seq'}, dimensions={2}, use_global_device_ids=true | all-gather | bytes 67584 | tf_op jit(solution)/shard_map/all_gather | solution.py:39
  86.6 11.0 %all_gather.15 = bf16[2,32,2048]{2,1,0:T(8,128)(2,1)S(1)} all-gather(bf16[2,8,2048]{2,1,0:T(8,128)(2,1)S(1)} %copy.148), channel_id=1, replica_groups=mesh['inst'=4,'seq'=32] {'inst'}, dimensions={1}, use_global_device_ids=true | all-gather | bytes 327680 | tf_op jit(solution)/shard_map/all_gather | solution.py:43
  98.3 11.9 %copy.180 = bf16[32,128,1024]{1,2,0:T(8,128)(2,1)} copy(bf16[32,128,1024]{2,1,0:T(8,128)(2,1)} %get-tuple-element.11) | data formatting | bytes 16777216
  112.7 1.5 copy.183
  114.2 1.7 gather_fusion.1
  115.9 6.3 bitcast_reduce_fusion
  122.4 1.3 select_reduce_fusion
  123.7 1.7 copy.152
  125.4 7.3 fusion.41
  134.8 65.4 %pmax.7 = f32[2,32,8,8]{1,3,2,0:T(8,128)S(1)} all-reduce(f32[2,32,8,8]{1,3,2,0:T(8,128)S(1)} %get-tuple-element.7), channel_id=1, replica_groups=mesh['inst'=4,'seq'=32] {'inst','seq'}, use_global_device_ids=true, to_apply=%region_6.7 | all-reduce | flops 4096 | bytes 32768 | tf_op jit(solution)/shard_map/pmax | solution.py:28
  201.2 2.3 convert_reduce_fusion.1
  203.8 1.4 fusion.18
  205.2 6.9 bitcast_multiply_fusion.1
  212.1 4.4 fusion.1
  216.4 2.6 copy.161
  219.0 2.8 reshape.224
  221.9 4.2 copy.162
  227.8 1.5 convert_reduce_fusion
  230.1 66.2 %all-reduce = f32[128,2,8,2]{2,3,1,0:T(2,128)S(1)} all-reduce(f32[128,2,8,2]{2,3,1,0:T(2,128)S(1)} %bitcast.123), channel_id=3, replica_groups=mesh['inst'=4,'seq'=32] {'inst','seq'}, use_global_device_ids=true, to_apply=%region_10.11.clone | all-reduce | flops 4096 | bytes 32768
  296.4 561.0 %reduce-scatter.2.cloned.1.call-done = f32[1,2,8,256]{3,2,1,0:T(8,128)} async-done(((f32[128,2,8,256]{3,2,1,0:T(8,128)}), f32[1,2,8,256]{3,2,1,0:T(8,128)}) %reduce-scatter.2.cloned.1.call-update) | async-done | bytes 16400 | tf_op jit(solution)/shard_map/reduce_scatter | solution.py:122
  857.4 1.4 fusion.22
  (72 shorter events, 11.8 us)
Async XLA Ops:
  7.2 103.1 %copy-start = (s32[32]{0:T(128)S(1)}, s32[32]{0:T(128)}, u32[]{:S(2)}) copy-start(s32[32]{0:T(128)} %param.11) | copy-start | bytes 388
  7.2 105.5 %all-gather.2.cloned.1.call-start = ((), (), s32[]{:S(2)}) async-start(), calls=%async_computation.1 | async-start | bytes 1310720 | tf_op jit(solution)/shard_map/all_gather | solution.py:42
  36.2 821.2 %reduce-scatter.2.cloned.1.call-start = ((), (), s32[]{:S(2)}) async-start(), calls=%async_computation.2 | async-start | bytes 2113536 | tf_op jit(solution)/shard_map/reduce_scatter | solution.py:122
  50.1 11.9 %copy-start.11 = (bf16[2,8,64]{2,1,0:T(8,128)(2,1)S(1)}, bf16[2,8,64]{2,1,0:T(8,128)(2,1)}, u32[]{:S(2)}) copy-start(bf16[2,8,64]{2,1,0:T(8,128)(2,1)} %param.10) | copy-start | bytes 6148
  97.6 0.7 copy-start.2
  98.3 12.7 %copy-start.7 = (s32[32,128]{1,0:T(8,128)S(1)}, s32[32,128]{1,0:T(8,128)}, u32[]{:S(2)}) copy-start(s32[32,128]{1,0:T(8,128)} %param.13) | copy-start | bytes 49156
  98.3 12.9 %copy-start.13 = (s32[2,32]{1,0:T(2,128)S(1)}, s32[2,32]{1,0:T(2,128)}, u32[]{:S(2)}) copy-start(s32[2,32]{1,0:T(2,128)} %param.14) | copy-start | bytes 772
  110.3 5.6 copy-start.8
  111.0 14.4 %copy-start.14 = (pred[2,2]{1,0:T(4,128)(4,1)}, pred[2,2]{1,0:T(4,128)(4,1)S(1)}, u32[]{:S(2)}) copy-start(pred[2,2]{1,0:T(4,128)(4,1)S(1)} %iota_compare_fusion.3) | copy-start | bytes 16
  111.8 4.1 copy-start.9
  122.4 10.4 %copy-start.5 = (f32[2,32,8,8]{1,3,2,0:T(8,128)}, f32[2,32,8,8]{1,3,2,0:T(8,128)S(1)}, u32[]{:S(2)}) copy-start(f32[2,32,8,8]{1,3,2,0:T(8,128)S(1)} %copy.155) | copy-start | bytes 49156
  125.4 75.8 %copy-start.10 = (pred[32]{0:T(512)(128)(4,1)S(1)}, pred[32]{0:T(512)(128)(4,1)}, u32[]{:S(2)}) copy-start(pred[32]{0:T(512)(128)(4,1)} %copy-done.9) | copy-start | bytes 100
  132.7 68.5 %copy-start.4 = (f32[2,32,8,8]{3,0,2,1:T(2,128)S(1)}, f32[2,32,8,8]{3,0,2,1:T(2,128)}, u32[]{:S(2)}) copy-start(f32[2,32,8,8]{3,0,2,1:T(2,128)} %get-tuple-element.14) | copy-start | bytes 49156
  132.7 68.5 %copy-start.6 = (f32[2,32,8,8]{1,3,2,0:T(8,128)S(1)}, f32[2,32,8,8]{1,3,2,0:T(8,128)}, u32[]{:S(2)}) copy-start(f32[2,32,8,8]{1,3,2,0:T(8,128)} %copy-done.5) | copy-start | bytes 49156
  226.0 0.7 copy-start.12
  226.0 0.8 copy-start.15
  226.0 1.0 copy-start.3
  227.0 631.8 %copy-start.1 = (s32[32]{0:T(128)S(1)}, s32[32]{0:T(128)}, u32[]{:S(2)}) copy-start(s32[32]{0:T(128)} %param.11) | copy-start | bytes 388
Sparse Core Ops, SparseCore 0:
  36.4 22.3 all-gather.1
  226.2 631.1 reduce-scatter.1
where the time goes:
time: 873 us; the launch traced here: 866 us
  waiting for transfers between devices  561 us (64%)
  blocking collectives  195 us (22%)
  local copies, waits for them, and re-layouts  57.6 us (7%)
  matrix products  27.2 us (3%)
  between operations  14.3 us (2%)
  other arithmetic  10 us (1%)
    reduce_scatter x1, waiting for transfers between devices, per_device(): lax.psum_scatter(num_flat, ('inst', 'seq'), scatter_dimension=0, tiled=True)  561 us
    unnamed x1, blocking collectives  66.2 us
    pmax x1, blocking collectives, rescaled(): peak_all = lax.pmax(peak_dev, ('inst', 'seq'))  65.4 us
    all_gather x1, blocking collectives, per_device(): lax.all_gather(queries, 'seq', axis=2, tiled=True)  29 us
    unnamed x37, local copies, waits for them, and re-layouts  27 us
    all_gather x1, blocking collectives, per_device(): lax.all_gather(new_kv, 'seq', axis=2, tiled=True)  23.9 us
  transfers between devices with their start and end apart: 2, of which 1 were waited for; matrix products, arithmetic and copies ran while one was open for 5% of the time, Pallas kernels for 0%

commit v1 on v0

v1 whole, which is shorter than its diff:
```python
import math

import jax
import jax.numpy as jnp
from jax import lax
from jax.experimental import pallas as pl
from jax.experimental.pallas import tpu as pltpu
from jax.sharding import PartitionSpec as P

MESH = pl.DeviceIdType.MESH
F32 = jnp.float32
BF16 = jnp.bfloat16
I32 = jnp.int32

N = 4
CHIPS = 64
SLOTS = 32
REQS = 32
LOW = -1e30
SCALE = 1.0 / math.sqrt(128)
UNROLL = 4
KV_PARTS = SLOTS // UNROLL


def iota(shape, dim):
    return lax.broadcasted_iota(I32, shape, dim)


def halves(first, second, late):
    lane = iota(first.shape, 1)
    if late is True:
        return jnp.where(lane < 64, pltpu.roll(first, 64, 1), second)
    if late is False:
        return jnp.where(lane < 64, first, pltpu.roll(second, 64, 1))
    low = jnp.where(late, pltpu.roll(first, 64, 1), first)
    high = jnp.where(late, second, pltpu.roll(second, 64, 1))
    return jnp.where(lane < 64, low, high)


def kernel(
    kv, q, nk, dev, slot, own_dev, own_row, lens, out, tail,
    kvb, gat, gq, gn, qr, wb, cb, mb, db, fb, mx, dx, mc, mt, dt, s32, r32, sb, rb, ss, rs, meta, smeta, codes,
    kv_sem, sa, ra, sbx, rbx, s_sib, r_sib, m_sems, s_chunk, r_chunk, all_sems, meta_sem,
):
    z = lax.axis_index("inst")
    c = lax.axis_index("seq")
    y, x, core = c // 8, (c // 2) % 4, c % 2
    me = z * 32 + c
    chip = z * 16 + y * 4 + x
    sib = 1 - core
    sibling = (z, y * 8 + x * 2 + sib)

    def place(pz, py, px):
        return (pz, py * 8 + px * 2 + core)

    def kv_copy(part):
        span = pl.ds(part * UNROLL, UNROLL)
        return pltpu.make_async_copy(kv.at[span], kvb.at[span], kv_sem.at[part])

    @pl.loop(0, KV_PARTS)
    def _(part):
        kv_copy(part).start()

    barrier = pltpu.get_barrier_semaphore()

    @pl.loop(1, CHIPS)
    def _(d):
        peer = place((z + d // 16) % 4, (y + (d // 4) % 4) % 4, (x + d % 4) % 4)
        pl.semaphore_signal(barrier, inc=1, device_id=peer, device_id_type=MESH)

    pl.semaphore_signal(barrier, inc=1, device_id=sibling, device_id_type=MESH)

    for s in range(2):
        own = q[s].astype(F32)
        gat[s, core, z, y, x] = jnp.concatenate([own[:, :128], own[:, 128:]], axis=0).astype(BF16)
    fresh = jnp.concatenate([nk[0].astype(F32), nk[1].astype(F32)], axis=1)
    gat[2, core, z, y, x] = jnp.concatenate([fresh, jnp.zeros((8, 128), F32)], axis=0).astype(BF16)

    pl.semaphore_wait(barrier, CHIPS)

    def moved(u, da, db):
        if u == 0:
            return z, (y + da) % 4, (x + db) % 4
        if u == 1:
            return (z + da) % 4, y, (x + db) % 4
        return (z + da) % 4, (y + db) % 4, x

    def plane_copy(u, d, at, to):
        block = gat.at[u, core, at[0], at[1], at[2]]
        return pltpu.make_async_remote_copy(
            src_ref=block, dst_ref=block, send_sem=sa.at[u, d], recv_sem=ra.at[u, d],
            device_id=place(*to), device_id_type=MESH,
        )

    for u in range(3):
        @pl.loop(1, 16)
        def _(d):
            plane_copy(u, d, (z, y, x), moved(u, d // 4, d % 4)).start()

    mine = jnp.where(dev[...] == me, slot[...], -1)
    code = iota((REQS, 128), 0) * 128 + iota((REQS, 128), 1) + 1
    for n in range(SLOTS):
        codes[n : n + 1, :] = jnp.sum(jnp.where(mine == n, code, 0), axis=0, keepdims=True)
    owned = jnp.where(own_dev[...] == me, own_row[...], -1)
    row_code = iota((2, REQS), 0) * REQS + iota((2, REQS), 1) + 1
    for e in range(8):
        hit = jnp.sum(jnp.where(owned == e, row_code, 0), axis=0, keepdims=True)
        codes[SLOTS + e : SLOTS + e + 1, :] = jnp.concatenate([hit, jnp.zeros((1, 96), I32)], axis=1)
    found = jnp.broadcast_to(jnp.sum(codes[...], axis=1, keepdims=True), (40, 128))
    held = found[:SLOTS]
    req_col = jnp.where(held > 0, jnp.minimum((held - 1) >> 7, REQS - 1), -1)
    rows, lanes = iota((SLOTS, 128), 0), iota((SLOTS, 128), 1)
    req_row = jnp.sum(jnp.where(rows == lanes, req_col, 0), axis=0, keepdims=True)
    req_row = jnp.where(lanes < SLOTS, jnp.broadcast_to(req_row, (SLOTS, 128)), -2)
    before = jnp.max(jnp.where((req_row == req_col) & (lanes < rows), lanes, -1), axis=1, keepdims=True)
    last = jnp.max(jnp.where(req_row == rows, lanes, -1), axis=1, keepdims=True)
    meta[:SLOTS] = jnp.where(
        lanes == 0, req_col, jnp.where(lanes == 1, held, jnp.where(lanes == 2, before, last))
    )
    meta[SLOTS:] = found[SLOTS:]
    meta_copy = pltpu.make_async_copy(meta, smeta, meta_sem)
    meta_copy.start()

    def axis_copy(u, k, at):
        if u == 0:
            block, to = gat.at[0, core, at], place((at + k) % 4, y, x)
        elif u == 1:
            block, to = gat.at[1, core, :, at], place(z, (at + k) % 4, x)
        else:
            block, to = gat.at[2, core, :, :, at], place(z, y, (at + k) % 4)
        return pltpu.make_async_remote_copy(
            src_ref=block, dst_ref=block, send_sem=sbx.at[u, k], recv_sem=rbx.at[u, k],
            device_id=to, device_id_type=MESH,
        )

    def sib_copy(u, of):
        block = gat.at[u, of]
        return pltpu.make_async_remote_copy(
            src_ref=block, dst_ref=block, send_sem=s_sib.at[u], recv_sem=r_sib.at[u],
            device_id=sibling, device_id_type=MESH,
        )

    here = (z, y, x)
    for u in range(3):
        @pl.loop(1, 16)
        def _(d):
            plane_copy(u, d, moved(u, 4 - d // 4, 4 - d % 4), here).wait_recv()

        for k in range(1, 4):
            axis_copy(u, k, here[u]).start()
    for u in range(3):
        for k in range(1, 4):
            axis_copy(u, k, (here[u] + 4 - k) % 4).wait_recv()
        sib_copy(u, core).start()
    meta_copy.wait()
    for u in range(3):
        sib_copy(u, sib).wait_recv()

    @pl.loop(0, 8)
    def _(k):
        of, i = k // 4, k % 4
        for j in range(16):
            for s in range(2):
                gq[of, i, pl.ds(j * 32 + s * 16, 16), :] = gat[s, of, i, j // 4, j % 4].astype(F32)
            gn[of, i, pl.ds(j * 8, 8), :] = gat[2, of, i, j // 4, j % 4].astype(F32)[:8]

    @pl.loop(0, REQS)
    def _(r):
        i, rl = r // 8, r % 8
        parts = [gq[of, i, pl.ds(rl, 64, stride=8), :].reshape(8, 8, 128) for of in range(2)]
        qr[r] = jnp.concatenate(parts, axis=1).astype(BF16)

    token = iota((128, 128), 0)
    blank = jnp.zeros((16, 128), BF16)

    @pl.loop(0, KV_PARTS)
    def _(part):
        kv_copy(part).wait()
        for e in range(UNROLL):
            n = part * UNROLL + e
            r = jnp.maximum(smeta[n, 0], 0)
            b = (jnp.maximum(smeta[n, 1], 1) - 1) % 128
            count = jnp.where(smeta[n, 1] > 0, lens[r] - b * 128, 0)
            heads = qr[r]
            score = jnp.zeros((128, 128), F32)
            for kt in range(4):
                rows_of = []
                for g in range(8):
                    if g == 2 * kt:
                        rows_of.append(jnp.concatenate([heads[g], blank], axis=1))
                    elif g == 2 * kt + 1:
                        rows_of.append(jnp.concatenate([blank, heads[g]], axis=1))
                    else:
                        rows_of.append(jnp.concatenate([blank, blank], axis=1))
                score = score + lax.dot_general(
                    kvb[n, :, kt * 256 : kt * 256 + 256], jnp.concatenate(rows_of, axis=0),
                    (((1,), (1,)), ((), ())), preferred_element_type=F32,
                )
            valid = token < count
            score = jnp.where(valid, score * SCALE, LOW)
            peak = jnp.max(score, axis=0, keepdims=True)
            w = jnp.where(valid, jnp.exp(score - peak), 0.0).astype(BF16).astype(F32)
            mb[pl.ds(n, 1), :] = peak
            db[pl.ds(n, 1), :] = jnp.sum(w, axis=0, keepdims=True)
            wb[n] = w.T.astype(BF16)

    rows = iota((REQS, 128), 0)
    top = jnp.full((REQS, 128), LOW, F32)
    for n in range(SLOTS):
        top = jnp.where(rows == smeta[n, 0], jnp.maximum(top, mb[n : n + 1, :]), top)
    mx[0] = top

    def pair_copy(buf, k):
        return pltpu.make_async_remote_copy(
            src_ref=buf.at[0], dst_ref=buf.at[1], send_sem=m_sems.at[2 * k], recv_sem=m_sems.at[2 * k + 1],
            device_id=sibling, device_id_type=MESH,
        )

    pair_copy(mx, 0).start()

    @pl.loop(0, KV_PARTS)
    def _(part):
        for e in range(UNROLL):
            n = part * UNROLL + e
            for kt in range(4):
                both = jnp.dot(
                    wb[n, kt * 32 : kt * 32 + 32, :], kvb[n, :, 1024 + kt * 256 : 1280 + kt * 256],
                    preferred_element_type=F32,
                )
                cb[n, kt * 32 : kt * 32 + 16, :] = both[:16, :128]
                cb[n, kt * 32 + 16 : kt * 32 + 32, :] = both[16:, 128:]

    pair_copy(mx, 0).wait_recv()
    chip_top = jnp.maximum(top, mx[1])
    mc[...] = chip_top
    den = jnp.zeros((REQS, 128), F32)
    fb[...] = jnp.zeros((128, 128), F32)
    for n in range(SLOTS):
        r = smeta[n, 0]
        factor = jnp.exp(mb[n : n + 1, :] - mc[pl.ds(jnp.maximum(r, 0), 1), :])
        fb[n : n + 1, :] = factor
        den = den + jnp.where(rows == r, factor * db[n : n + 1, :], 0.0)
    dx[0] = den
    pair_copy(dx, 1).start()
    fb[...] = fb[...].T

    def chunk_copy(kt):
        return pltpu.make_async_remote_copy(
            src_ref=s32.at[sib, :, pl.ds(pl.multiple_of(kt * 128, 128), 128), :], dst_ref=r32.at[kt],
            send_sem=s_chunk.at[kt], recv_sem=r_chunk.at[kt], device_id=sibling, device_id_type=MESH,
        )

    @pl.loop(0, 4)
    def _(k):
        kt = (y + k) % 4
        span = pl.ds(pl.multiple_of(kt * 32, 32), 32)
        scales = fb[span, :]
        for n in range(SLOTS):
            prev = smeta[n, 2]
            earlier = jnp.where(prev >= 0, cb[jnp.maximum(prev, 0), span, :], 0.0)
            cb[n, span, :] = cb[n, span, :] * scales[:, n : n + 1] + earlier
        for r in range(REQS):
            end = smeta[r, 3]
            sums = jnp.where(end >= 0, cb[jnp.maximum(end, 0), span, :], 0.0)
            for xh in range(2):
                for of in range(2):
                    start = kt * 128 + xh * 64 + r % 8
                    s32[of, r // 8, pl.ds(start, 8, stride=8), :] = sums[xh * 16 + of * 8 : xh * 16 + of * 8 + 8]
        chunk_copy(kt).start()

    pair_copy(dx, 1).wait_recv()
    chip_den = dx[0] + dx[1]
    pad = jnp.zeros((96, 128), F32)
    mt[...] = jnp.concatenate([chip_top, pad], axis=0).T
    dt[...] = jnp.concatenate([chip_den, pad], axis=0).T
    lane8 = iota((8, 128), 1)
    for i in range(4):
        for xl in range(2):
            packed = jnp.zeros((8, 128), F32)
            for t in range(4):
                for w, src in ((0, mt), (1, dt)):
                    got = src[pl.ds(core * 8 + xl * 4 + t, 8, stride=16), :]
                    to = w * 32 + t * 8
                    got = pltpu.roll(got, (to - 8 * i) % 128, 1)
                    packed = jnp.where((lane8 >= to) & (lane8 < to + 8), got, packed)
            for g in range(8):
                ss[i * 16 + g * 2 + xl] = packed[g : g + 1, :]

    def block_copy(to_chip, to):
        return pltpu.make_async_remote_copy(
            src_ref=sb.at[to_chip], dst_ref=rb.at[chip], send_sem=all_sems.at[0], recv_sem=all_sems.at[1],
            device_id=to, device_id_type=MESH,
        )

    def side_copy(to_chip, to):
        return pltpu.make_async_remote_copy(
            src_ref=ss.at[to_chip], dst_ref=rs.at[chip], send_sem=all_sems.at[2], recv_sem=all_sems.at[3],
            device_id=to, device_id_type=MESH,
        )

    rs[chip] = ss[chip]

    @pl.loop(0, 4)
    def _(k):
        kt = (y + k) % 4
        chunk_copy(kt).wait_recv()
        for i in range(4):
            for j in range(4):
                at = pl.ds(pl.multiple_of(kt * 128 + j * 32, 32), 32)
                total = s32[core, i, at, :] + r32[kt, i, j * 32 : j * 32 + 32, :]
                sb[i * 16 + kt * 4 + j] = total.astype(BF16)

        @pl.loop(0, 16)
        def _(d):
            pz, px = (z + d // 4) % 4, (x + d % 4) % 4
            to_chip, to = pz * 16 + kt * 4 + px, place(pz, kt, px)

            @pl.when(k * 16 + d > 0)
            def _():
                block_copy(to_chip, to).start()
                side_copy(to_chip, to).start()

    rb[chip] = sb[chip]

    for e in range(4):
        found_row = smeta[SLOTS + e, 0]
        which = jnp.maximum(found_row - 1, 0)
        late, r = which // 32, which % 32
        pair = [gn[of, r // 8, pl.ds(r % 8, 16, stride=8), :] for of in range(2)]
        tail[e] = jnp.where(found_row > 0, halves(pair[0], pair[1], late > 0), 0.0).astype(BF16)

    head = y * 2 + x // 2
    new_rows = []
    for at in (head, head + 8):
        pair = [gn[of, z, pl.ds(pl.multiple_of(at * 8, 8), 8), :] for of in range(2)]
        new_rows.append([halves(pair[0], pair[1], late) for late in (False, True)])
    new_m, new_den, new_num = [], [], []
    for t in range(4):
        mine_q = q[t // 2].astype(F32)[:, (t % 2) * 128 : (t % 2) * 128 + 128]
        found_scores = [
            jnp.sum(mine_q * new_rows[0][j], axis=1, keepdims=True) * SCALE for j in range(t // 2 + 1)
        ]
        peak = found_scores[0]
        for more in found_scores[1:]:
            peak = jnp.maximum(peak, more)
        ws = [jnp.exp(v - peak).astype(BF16).astype(F32) for v in found_scores]
        new_m.append(peak)
        new_den.append(sum(ws[1:], ws[0]))
        num = ws[0] * new_rows[1][0]
        for j in range(1, len(ws)):
            num = num + ws[j] * new_rows[1][j]
        new_num.append(num)
    new_m = jnp.concatenate(new_m, axis=0)
    new_den = jnp.concatenate(new_den, axis=0)
    new_num = jnp.concatenate(new_num, axis=0)

    most = pl.ds(0, CHIPS - 1)
    all_blocks = pltpu.make_async_remote_copy(
        src_ref=sb.at[most], dst_ref=rb.at[most], send_sem=all_sems.at[0], recv_sem=all_sems.at[1],
        device_id=sibling, device_id_type=MESH,
    )
    all_sides = pltpu.make_async_remote_copy(
        src_ref=ss.at[most], dst_ref=rs.at[most], send_sem=all_sems.at[2], recv_sem=all_sems.at[3],
        device_id=sibling, device_id_type=MESH,
    )
    all_sides.wait_recv()
    side = rs[...].reshape(CHIPS, 128)
    side = jnp.concatenate([side, jnp.zeros((128 - CHIPS, 128), F32)], axis=0).T
    side_m, side_den = side[0:32, :CHIPS], side[32:64, :CHIPS]
    final_m = jnp.maximum(jnp.max(side_m, axis=1, keepdims=True), new_m)
    scales = jnp.exp(side_m - final_m)
    new_scale = jnp.exp(new_m - final_m)
    final_den = jnp.sum(scales * side_den, axis=1, keepdims=True) + new_den * new_scale
    total = new_num * new_scale
    all_blocks.wait_recv()
    for k in range(CHIPS):
        total = total + scales[:, k : k + 1] * rb[k].astype(F32)
    result = total / final_den
    for t in range(4):
        out[t // 2, :, (t % 2) * 128 : (t % 2) * 128 + 128] = result[t * 8 : t * 8 + 8].astype(BF16)

    all_blocks.wait_send()
    all_sides.wait_send()
    for u in range(3):
        @pl.loop(1, 16)
        def _(d):
            plane_copy(u, d, here, moved(u, d // 4, d % 4)).wait_send()

        for k in range(1, 4):
            axis_copy(u, k, here[u]).wait_send()
        sib_copy(u, core).wait_send()
    pair_copy(mx, 0).wait_send()
    pair_copy(dx, 1).wait_send()

    @pl.loop(0, 4)
    def _(k):
        chunk_copy(k).wait_send()


def per_device(kv_pool, queries, new_kv, lengths, block_dev, block_slot, owner_dev, owner_row):
    vmem = pl.BlockSpec(memory_space=pltpu.VMEM)
    dma = pltpu.SemaphoreType.DMA
    result, tail = pl.pallas_call(
        kernel,
        out_shape=(
            jax.ShapeDtypeStruct((2, 8, 256), BF16),
            jax.ShapeDtypeStruct((4, 16, 128), BF16),
        ),
        in_specs=[pl.BlockSpec(memory_space=pl.ANY)] + [vmem] * 6 + [pl.BlockSpec(memory_space=pltpu.SMEM)],
        out_specs=(vmem, vmem),
        scratch_shapes=[
            pltpu.VMEM((SLOTS, 128, 2048), BF16),
            pltpu.VMEM((3, 2, 4, 4, 4, 16, 128), BF16),
            pltpu.VMEM((2, 4, 512, 128), F32),
            pltpu.VMEM((2, 4, 128, 128), F32),
            pltpu.VMEM((REQS, 8, 16, 128), BF16),
            pltpu.VMEM((SLOTS, 128, 128), BF16),
            pltpu.VMEM((SLOTS, 128, 128), F32),
            pltpu.VMEM((SLOTS, 128), F32),
            pltpu.VMEM((SLOTS, 128), F32),
            pltpu.VMEM((128, 128), F32),
            pltpu.VMEM((2, REQS, 128), F32),
            pltpu.VMEM((2, REQS, 128), F32),
            pltpu.VMEM((REQS, 128), F32),
            pltpu.VMEM((128, 128), F32),
            pltpu.VMEM((128, 128), F32),
            pltpu.VMEM((2, 4, 512, 128), F32),
            pltpu.VMEM((4, 4, 128, 128), F32),
            pltpu.VMEM((CHIPS, 32, 128), BF16),
            pltpu.VMEM((CHIPS, 32, 128), BF16),
            pltpu.VMEM((CHIPS, 1, 128), F32),
            pltpu.VMEM((CHIPS, 1, 128), F32),
            pltpu.VMEM((40, 128), I32),
            pltpu.SMEM((40, 128), I32),
            pltpu.VMEM((40, 128), I32),
            dma((KV_PARTS,)),
            dma((3, 16)),
            dma((3, 16)),
            dma((3, 4)),
            dma((3, 4)),
            dma((3,)),
            dma((3,)),
            dma((4,)),
            dma((4,)),
            dma((4,)),
            dma((4,)),
            dma,
        ],
        compiler_params=pltpu.CompilerParams(
            collective_id=0, has_side_effects=True, vmem_limit_bytes=56 * 1024 * 1024
        ),
    )(kv_pool, queries, new_kv, block_dev, block_slot, owner_dev, owner_row, lengths)
    return result, tail.reshape(4, 2048)


def solution(mesh):
    placed = (
        P(("inst", "seq"), None, None),
        P(None, "inst", "seq"),
        P(None, "inst", "seq"),
        P(),
        P(),
        P(),
        P(),
        P(),
    )
    return jax.shard_map(
        per_device,
        mesh=mesh,
        in_specs=placed,
        out_specs=(P(None, "inst", "seq"), P(("inst", "seq"), None)),
        check_vma=False,
    )
```

time: 873 us -> 50 us (0.06)
  waiting for transfers between devices: 561 us -> 0 us
  blocking collectives: 195 us -> 0 us
  local copies, waits for them, and re-layouts: 57.6 us -> 2.62 us
  Pallas kernels: 0 us -> 46.4 us
  matrix products: 27.2 us -> 0 us
  between operations: 14.3 us -> 0.64 us
  other arithmetic: 10 us -> 0 us
    reduce_scatter x1 -> x0, waiting for transfers between devices: 561 us -> none  [per_device(): lax.psum_scatter(num_flat, ('inst', 'seq'), scatter_dimension=0, tiled=True)]
    unnamed x1 -> x0, blocking collectives: 66.2 us -> none
    pmax x1 -> x0, blocking collectives: 65.4 us -> none  [rescaled(): peak_all = lax.pmax(peak_dev, ('inst', 'seq'))]
    all_gather x3 -> x0, blocking collectives: 63.8 us -> none  [the longest x1 29 us: per_device(): lax.all_gather(queries, 'seq', axis=2, tiled=True)]
    pallas_call x0 -> x1, Pallas kernels: none -> 46.4 us  [per_device(): pl.pallas_call(kernel, out_shape=(jax.ShapeDtypeStruct((2, 8, 256), BF16)...]
    dot_general x7 -> x0, matrix products: 27.2 us -> none  [the longest x1 7.34 us: per_device(): jnp.einsum('srgqd,jrgd->srgqj', q_heads, row_parts[:, :, 0], preferred_el...]
    unnamed x37 -> x2, local copies, waits for them, and re-layouts: 27 us -> 2.62 us
    slice x2 -> x0, local copies, waits for them, and re-layouts: 12.9 us -> none  [the longest x1 12.1 us: per_device(): key_rows = kv_pool[:, :, :KVH * HD].reshape(slot_count, block_len, KVH, HD)]
  transfers between devices with their start and end apart: 2 -> 0, of which waited for: 1 -> 0; matrix products, arithmetic and copies ran while one was open for 5% -> 0% of each run, Pallas kernels for 0% -> 0%
where the time goes in v1:
time: 50 us; the launch traced here: 49.7 us
  Pallas kernels  46.4 us (93%)
  local copies, waits for them, and re-layouts  2.62 us (5%)
  between operations  0.64 us (1%)
    pallas_call x1, Pallas kernels, per_device(): pl.pallas_call(kernel, out_shape=(jax.ShapeDtypeStruct((2, 8, 256), BF16)...  46.4 us
    unnamed x2, local copies, waits for them, and re-layouts  2.62 us

profile of v1, /device:TPU:1, one launch (start us, length us, event | category | flops | bytes accessed | tf_op | source)
XLA Modules:
  0.0 49.7 jit_solution(2249875180513116726)
XLA Ops:
  0.6 46.4 %shard_map.95 = (bf16[2,8,256]{2,1,0:T(8,128)(2,1)}, bf16[4,16,128]{2,1,0:T(8,128)(2,1)}) custom-call(bf16[32,128,2048]{2,1,0:T(8,128)(2,1)} %kv.1, bf16[2,8,256]{2,1,0:T(8,128)(2,1)} %q.1, bf16[2,8,64]{2,1,0:T(8,128)(2,1)} %nk.1, s32[32,128]{1,0:T(8,128)} %dev.1, s32[32,128]{1,0:T(8,128)} %slot.1, s32[2,32]{1,0:T(2,128)} %own_dev.1, s32[2,32]{1,0:T(2,128)} %own_row.1, ...), custom_call_target="tpu_custom_call" | custom-call | tf_op jit(solution)/shard_map/pallas_call | solution.py:403
  47.1 1.3 %copy.12 = bf16[1,4,16,128]{3,1,2,0:T(4,128)(2,1)} copy(bf16[1,4,16,128]{3,2,1,0:T(8,128)(2,1)} %bitcast.5) | data formatting | bytes 32768
  48.4 1.3 %copy.14 = bf16[2,8,256]{2,1,0:T(8,128)(2,1)} copy(bf16[2,8,256]{2,1,0:T(8,128)(2,1)} %get-tuple-element.8) | data formatting | bytes 16384

commit v2 on v1

v2 whole, which is shorter than its diff:
```python
import math

import jax
import jax.numpy as jnp
from jax import lax
from jax.experimental import pallas as pl
from jax.experimental.pallas import tpu as pltpu
from jax.sharding import PartitionSpec as P

MESH = pl.DeviceIdType.MESH
F32 = jnp.float32
BF16 = jnp.bfloat16
I32 = jnp.int32

N = 4
CHIPS = 64
SLOTS = 32
REQS = 32
LOW = -1e30
SCALE = 1.0 / math.sqrt(128)
UNROLL = 4
GROUP = 8
KV_PARTS = SLOTS // UNROLL
FAR_FIRST = (3, 2, 1, 0)


def iota(shape, dim):
    return lax.broadcasted_iota(I32, shape, dim)


def halves(first, second, late):
    lane = iota(first.shape, 1)
    if late is True:
        return jnp.where(lane < 64, pltpu.roll(first, 64, 1), second)
    if late is False:
        return jnp.where(lane < 64, first, pltpu.roll(second, 64, 1))
    low = jnp.where(late, pltpu.roll(first, 64, 1), first)
    high = jnp.where(late, second, pltpu.roll(second, 64, 1))
    return jnp.where(lane < 64, low, high)


def kernel(
    kv, q, nk, dev, slot, own_dev, own_row, lens, out, tail,
    kvb, gat, gnb, gq, gn, wb, cb, mb, db, fb, mx, lift, mc, mt, dt, s32, r32, sb, rb, ss, rs, tl, meta, smeta, codes,
    k_sem, v_sem, sg, rg, s_sib, r_sib, m_sems, s_chunk, r_chunk, all_sems, meta_sem,
):
    z = lax.axis_index("inst")
    c = lax.axis_index("seq")
    y, x, core = c // 8, (c // 2) % 4, c % 2
    me = z * 32 + c
    chip = z * 16 + y * 4 + x
    sib = 1 - core
    sibling = (z, y * 8 + x * 2 + sib)

    def place(pz, py, px):
        return (pz, py * 8 + px * 2 + core)

    def offset(d):
        return (z + d // 16) % 4, (y + (d // 4) % 4) % 4, (x + d % 4) % 4

    barrier = pltpu.get_barrier_semaphore()

    @pl.loop(1, CHIPS)
    def _(d):
        pl.semaphore_signal(barrier, inc=1, device_id=place(*offset(d)), device_id_type=MESH)

    pl.semaphore_signal(barrier, inc=1, device_id=sibling, device_id_type=MESH)

    def key_copy(part):
        span = pl.ds(part * UNROLL, UNROLL)
        cols = pl.ds(0, 1024)
        return pltpu.make_async_copy(kv.at[span, :, cols], kvb.at[span, :, cols], k_sem.at[part])

    def value_copy(part):
        span = pl.ds(part * UNROLL, UNROLL)
        cols = pl.ds(1024, 1024)
        return pltpu.make_async_copy(kv.at[span, :, cols], kvb.at[span, :, cols], v_sem.at[part])

    @pl.loop(0, KV_PARTS)
    def _(part):
        key_copy(part).start()

    spot = y * 4 + x
    own = [q[s].astype(F32) for s in range(2)]
    gat[core, z, spot] = jnp.concatenate(
        [own[0][:, :128], own[0][:, 128:], own[1][:, :128], own[1][:, 128:]], axis=0
    ).astype(BF16)
    fresh = jnp.concatenate([nk[0].astype(F32), nk[1].astype(F32)], axis=1)
    gnb[core, chip] = jnp.concatenate([fresh, jnp.zeros((8, 128), F32)], axis=0).astype(BF16)

    pl.semaphore_wait(barrier, CHIPS)

    def query_copy(d):
        block = gat.at[core, z, spot]
        return pltpu.make_async_remote_copy(
            src_ref=block, dst_ref=block, send_sem=sg.at[d // 16], recv_sem=rg.at[d // 16],
            device_id=place(*offset(d)), device_id_type=MESH,
        )

    def fresh_copy(d):
        block = gnb.at[core, chip]
        return pltpu.make_async_remote_copy(
            src_ref=block, dst_ref=block, send_sem=sg.at[4], recv_sem=rg.at[4],
            device_id=place(*offset(d)), device_id_type=MESH,
        )

    def plane_wait(dz):
        at = (z + 4 - dz) % 4
        block = gat.at[core, at] if dz else gat.at[core, at, pl.ds(0, 15)]
        return pltpu.make_async_remote_copy(
            src_ref=block, dst_ref=block, send_sem=sg.at[dz], recv_sem=rg.at[dz],
            device_id=sibling, device_id_type=MESH,
        )

    def sib_copy(dz, of):
        block = gat.at[of, (z + 4 - dz) % 4]
        return pltpu.make_async_remote_copy(
            src_ref=block, dst_ref=block, send_sem=s_sib.at[dz], recv_sem=r_sib.at[dz],
            device_id=sibling, device_id_type=MESH,
        )

    def sib_fresh(of):
        block = gnb.at[of]
        return pltpu.make_async_remote_copy(
            src_ref=block, dst_ref=block, send_sem=s_sib.at[4], recv_sem=r_sib.at[4],
            device_id=sibling, device_id_type=MESH,
        )

    def fresh_wait():
        block = gnb.at[core, pl.ds(0, CHIPS - 1)]
        return pltpu.make_async_remote_copy(
            src_ref=block, dst_ref=block, send_sem=sg.at[4], recv_sem=rg.at[4],
            device_id=sibling, device_id_type=MESH,
        )

    @pl.loop(0, CHIPS - 1)
    def _(d):
        query_copy(CHIPS - 1 - d).start()

    @pl.loop(0, KV_PARTS)
    def _(part):
        value_copy(part).start()

    @pl.loop(1, CHIPS)
    def _(d):
        fresh_copy(d).start()

    mine = jnp.where(dev[...] == me, slot[...], -1)
    code = iota((REQS, 128), 0) * 128 + iota((REQS, 128), 1) + 1

    @pl.loop(0, SLOTS // 4)
    def _(group):
        for e in range(4):
            n = group * 4 + e
            codes[pl.ds(n, 1), :] = jnp.sum(jnp.where(mine == n, code, 0), axis=0, keepdims=True)

    owned = jnp.where(own_dev[...] == me, own_row[...], -1)
    row_code = iota((2, REQS), 0) * REQS + iota((2, REQS), 1) + 1
    pad_row = jnp.zeros((1, 96), I32)
    for e in range(4):
        hit = jnp.sum(jnp.where(owned == e, row_code, 0), axis=0, keepdims=True)
        codes[SLOTS + e : SLOTS + e + 1, :] = jnp.concatenate([hit, pad_row], axis=1)
    codes[SLOTS + 4 :, :] = jnp.zeros((4, 128), I32)

    found = jnp.broadcast_to(jnp.sum(codes[...], axis=1, keepdims=True), (40, 128))
    held = found[:SLOTS]
    req_col = jnp.where(held > 0, jnp.minimum((held - 1) >> 7, REQS - 1), -1)
    rows, lanes = iota((SLOTS, 128), 0), iota((SLOTS, 128), 1)
    req_row = jnp.sum(jnp.where(rows == lanes, req_col, 0), axis=0, keepdims=True)
    req_row = jnp.where(lanes < SLOTS, jnp.broadcast_to(req_row, (SLOTS, 128)), -2)
    before = jnp.max(jnp.where((req_row == req_col) & (lanes < rows), lanes, -1), axis=1, keepdims=True)
    last = jnp.max(jnp.where(req_row == rows, lanes, -1), axis=1, keepdims=True)
    meta[:SLOTS] = jnp.where(
        lanes == 0, req_col, jnp.where(lanes == 1, held, jnp.where(lanes == 2, before, last))
    )
    meta[SLOTS:] = found[SLOTS:]
    meta_copy = pltpu.make_async_copy(meta, smeta, meta_sem)
    meta_copy.start()

    def widen(of, dz):
        i = (z + 4 - dz) % 4

        @pl.loop(0, 4)
        def _(group):
            for e in range(4):
                j = group * 4 + e
                gq[of, i, pl.ds(j * 32, 32), :] = gat[of, i, j].astype(F32)

    for dz in FAR_FIRST:
        plane_wait(dz).wait_recv()
        sib_copy(dz, core).start()
        widen(core, dz)
    meta_copy.wait()
    for dz in FAR_FIRST:
        sib_copy(dz, sib).wait_recv()
        widen(sib, dz)

    token = iota((128, 128), 0)
    head_of = iota((16, 128), 1) // 16
    pick = [jnp.where(head_of == g, 1.0, 0.0).astype(BF16) for g in range(8)]

    @pl.loop(0, KV_PARTS)
    def _(part):
        key_copy(part).wait()
        for e in range(UNROLL):
            n = part * UNROLL + e
            r = jnp.maximum(smeta[n, 0], 0)
            b = (jnp.maximum(smeta[n, 1], 1) - 1) % 128
            count = jnp.where(smeta[n, 1] > 0, lens[r] - b * 128, 0)
            parts = [gq[of, r // 8, pl.ds(r % 8, 64, stride=8), :].reshape(8, 8, 128) for of in range(2)]
            turned = jnp.concatenate(parts, axis=1).reshape(128, 128).T.astype(BF16).reshape(8, 16, 128)
            score = jnp.zeros((128, 128), F32)
            for kt in range(4):
                pair = [(turned * pick[g]).reshape(128, 128) for g in (2 * kt, 2 * kt + 1)]
                score = score + jnp.dot(
                    kvb[n, :, kt * 256 : kt * 256 + 256], jnp.concatenate(pair, axis=0),
                    preferred_element_type=F32,
                )
            valid = token < count
            score = jnp.where(valid, score * SCALE, LOW)
            peak = jnp.max(score, axis=0, keepdims=True)
            w = jnp.where(valid, jnp.exp(score - peak), 0.0).astype(BF16)
            mb[pl.ds(n, 1), :] = peak
            db[pl.ds(n, 1), :] = jnp.sum(w.astype(F32), axis=0, keepdims=True)
            wb[n] = w.T

    fresh_wait().wait_recv()
    sib_fresh(core).start()

    rows = iota((REQS, 128), 0)
    top = jnp.full((REQS, 128), LOW, F32)

    @pl.loop(0, SLOTS // 4, init_carry=top)
    def top(group, most):
        for e in range(4):
            n = group * 4 + e
            most = jnp.where(rows == smeta[n, 0], jnp.maximum(most, mb[pl.ds(n, 1), :]), most)
        return most

    mc[...] = top
    fb[...] = jnp.zeros((128, 128), F32)

    @pl.loop(0, SLOTS // 4, init_carry=jnp.zeros((REQS, 128), F32))
    def den(group, sums):
        for e in range(4):
            n = group * 4 + e
            r = smeta[n, 0]
            factor = jnp.exp(mb[pl.ds(n, 1), :] - mc[pl.ds(jnp.maximum(r, 0), 1), :])
            fb[pl.ds(n, 1), :] = factor
            sums = sums + jnp.where(rows == r, factor * db[pl.ds(n, 1), :], 0.0)
        return sums

    fb[...] = fb[...].T
    mx[0, 0] = top
    mx[0, 1] = den
    pair_copy = pltpu.make_async_remote_copy(
        src_ref=mx.at[0], dst_ref=mx.at[1], send_sem=m_sems.at[0], recv_sem=m_sems.at[1],
        device_id=sibling, device_id_type=MESH,
    )
    pair_copy.start()

    @pl.loop(0, KV_PARTS)
    def _(part):
        value_copy(part).wait()

    def turn(k):
        return (y + k) % 4

    def product(k, n):
        kt = turn(k)
        both = jnp.dot(
            wb[n, pl.ds(pl.multiple_of(kt * 32, 32), 32), :],
            kvb[n, :, pl.ds(pl.multiple_of(1024 + kt * 256, 256), 256)],
            preferred_element_type=F32,
        )
        return jnp.concatenate([both[:16, :128], both[16:, 128:]], axis=0)

    def chunk_copy(k):
        kt = turn(k)
        return pltpu.make_async_remote_copy(
            src_ref=s32.at[sib, :, pl.ds(pl.multiple_of(kt * 128, 128), 128), :], dst_ref=r32.at[k],
            send_sem=s_chunk.at[k], recv_sem=r_chunk.at[k], device_id=sibling, device_id_type=MESH,
        )

    def block_copy(to_chip, to):
        return pltpu.make_async_remote_copy(
            src_ref=sb.at[to_chip], dst_ref=rb.at[chip], send_sem=all_sems.at[0], recv_sem=all_sems.at[1],
            device_id=to, device_id_type=MESH,
        )

    def side_copy(to_chip, to):
        return pltpu.make_async_remote_copy(
            src_ref=ss.at[to_chip], dst_ref=rs.at[chip], send_sem=all_sems.at[2], recv_sem=all_sems.at[3],
            device_id=to, device_id_type=MESH,
        )

    def merge(k):
        kt = turn(k)
        chunk_copy(k).wait_recv()
        shift = (128 - (kt * 32 + core * 8)) % 128

        @pl.loop(0, 4)
        def _(i):
            mine_f, other_f = [pltpu.roll(lift[f, pl.ds(i * 8, 8), :], shift, 1) for f in range(2)]
            for j in range(4):
                total = []
                for t in range(4):
                    lane = (j // 2) * 16 + (j % 2) * 4 + t
                    at = pl.ds(pl.multiple_of(kt * 128 + j * 32 + t * 8, 8), 8)
                    there = r32[k, i, j * 32 + t * 8 : j * 32 + t * 8 + 8, :]
                    total.append(
                        s32[core, i, at, :] * mine_f[:, lane : lane + 1] + there * other_f[:, lane : lane + 1]
                    )
                sb[i * 16 + kt * 4 + j] = jnp.concatenate(total, axis=0).astype(BF16)

    def meet():
        pair_copy.wait_recv()
        chip_top = jnp.maximum(top, mx[1, 0])
        mine_f, other_f = jnp.exp(top - chip_top), jnp.exp(mx[1, 0] - chip_top)
        chip_den = den * mine_f + mx[1, 1] * other_f
        pad = jnp.zeros((96, 128), F32)
        mt[...] = jnp.concatenate([chip_top, pad], axis=0).T
        dt[...] = jnp.concatenate([chip_den, pad], axis=0).T
        lane8 = iota((8, 128), 1)
        for i in range(4):
            for xl in range(2):
                packed = jnp.zeros((8, 128), F32)
                for t in range(4):
                    for w, src in ((0, mt), (1, dt)):
                        got = src[pl.ds(core * 8 + xl * 4 + t, 8, stride=16), :]
                        to = w * 32 + t * 8
                        got = pltpu.roll(got, (to - 8 * i) % 128, 1)
                        packed = jnp.where((lane8 >= to) & (lane8 < to + 8), got, packed)
                for g in range(8):
                    ss[i * 16 + g * 2 + xl] = packed[g : g + 1, :]
        rs[chip] = ss[chip]
        lift[0] = mine_f
        lift[1] = other_f

    def send(k):
        kt = turn(k)

        @pl.loop(0, 16)
        def _(d):
            pz, px = (z + d // 4) % 4, (x + d % 4) % 4
            to_chip, to = pz * 16 + kt * 4 + px, place(pz, kt, px)

            @pl.when(k * 16 + d > 0)
            def _():
                block_copy(to_chip, to).start()
                side_copy(to_chip, to).start()

    @pl.loop(0, 5)
    def _(k):
        kt = turn(k)

        @pl.when(k < 4)
        def _():
            @pl.loop(0, SLOTS // GROUP)
            def _(group):
                scales = fb[pl.ds(pl.multiple_of(kt * 32, 32), 32), :]
                scales = pltpu.roll(scales, (128 - group * GROUP) % 128, 1)
                for e in range(GROUP):
                    n = group * GROUP + e
                    prev = smeta[n, 2]
                    earlier = jnp.where(prev >= 0, cb[jnp.maximum(prev, 0)], 0.0)
                    cb[n] = product(k, n) * scales[:, e : e + 1] + earlier

            @pl.loop(0, 4)
            def _(i):
                for rl in range(8):
                    end = smeta[i * 8 + rl, 3]
                    sums = jnp.where(end >= 0, cb[jnp.maximum(end, 0)], 0.0)
                    for xh in range(2):
                        for of in range(2):
                            start = kt * 128 + xh * 64 + rl
                            s32[of, i, pl.ds(start, 8, stride=8), :] = sums[xh * 16 + of * 8 : xh * 16 + of * 8 + 8]

            chunk_copy(k).start()

        @pl.when(k == 1)
        def _():
            meet()

        @pl.when(k > 0)
        def _():
            merge(k - 1)
            send(k - 1)

    rb[chip] = sb[chip]

    sib_fresh(sib).wait_recv()
    @pl.loop(0, 8)
    def _(k):
        of, i = k // 4, k % 4
        for j in range(16):
            gn[of, i, j * 8 : j * 8 + 8, :] = gnb[of, i * 16 + j].astype(F32)[:8]

    @pl.loop(0, 4)
    def _(e):
        found_row = smeta[SLOTS + e, 0]
        which = jnp.maximum(found_row - 1, 0)
        late, r = which // 32, which % 32
        pair = [gn[of, r // 8, pl.ds(r % 8, 16, stride=8), :] for of in range(2)]
        tl[pl.ds(pl.multiple_of(e * 16, 16), 16), :] = jnp.where(found_row > 0, halves(pair[0], pair[1], late > 0), 0.0)
    for j in range(16):
        tail[:, j * 128 : j * 128 + 128] = tl[pl.ds(j, 4, stride=16), :].astype(BF16)

    head = y * 2 + x // 2
    new_rows = []
    for at in (head, head + 8):
        pair = [gn[of, z, pl.ds(pl.multiple_of(at * 8, 8), 8), :] for of in range(2)]
        new_rows.append([halves(pair[0], pair[1], late) for late in (False, True)])
    new_m, new_den, new_num = [], [], []
    for t in range(4):
        mine_q = q[t // 2].astype(F32)[:, (t % 2) * 128 : (t % 2) * 128 + 128]
        found_scores = [
            jnp.sum(mine_q * new_rows[0][j], axis=1, keepdims=True) * SCALE for j in range(t // 2 + 1)
        ]
        peak = found_scores[0]
        for more in found_scores[1:]:
            peak = jnp.maximum(peak, more)
        ws = [jnp.exp(v - peak).astype(BF16).astype(F32) for v in found_scores]
        new_m.append(peak)
        new_den.append(sum(ws[1:], ws[0]))
        num = ws[0] * new_rows[1][0]
        for j in range(1, len(ws)):
            num = num + ws[j] * new_rows[1][j]
        new_num.append(num)
    new_m = jnp.concatenate(new_m, axis=0)
    new_den = jnp.concatenate(new_den, axis=0)
    new_num = jnp.concatenate(new_num, axis=0)

    most = pl.ds(0, CHIPS - 1)
    all_blocks = pltpu.make_async_remote_copy(
        src_ref=sb.at[most], dst_ref=rb.at[most], send_sem=all_sems.at[0], recv_sem=all_sems.at[1],
        device_id=sibling, device_id_type=MESH,
    )
    all_sides = pltpu.make_async_remote_copy(
        src_ref=ss.at[most], dst_ref=rs.at[most], send_sem=all_sems.at[2], recv_sem=all_sems.at[3],
        device_id=sibling, device_id_type=MESH,
    )
    all_sides.wait_recv()
    side = rs[...].reshape(CHIPS, 128)
    side = jnp.concatenate([side, jnp.zeros((128 - CHIPS, 128), F32)], axis=0).T
    side_m, side_den = side[0:32, :CHIPS], side[32:64, :CHIPS]
    final_m = jnp.maximum(jnp.max(side_m, axis=1, keepdims=True), new_m)
    scales = jnp.exp(side_m - final_m)
    new_scale = jnp.exp(new_m - final_m)
    final_den = jnp.sum(scales * side_den, axis=1, keepdims=True) + new_den * new_scale
    total = new_num * new_scale
    all_blocks.wait_recv()
    scales = jnp.concatenate([scales, jnp.zeros((32, 128 - CHIPS), F32)], axis=1)

    @pl.loop(0, CHIPS // 8, init_carry=(total, scales))
    def total_and_scales(group, carry):
        total, scales = carry
        for e in range(8):
            total = total + scales[:, e : e + 1] * rb[group * 8 + e].astype(F32)
        return total, pltpu.roll(scales, 120, 1)

    total = total_and_scales[0]
    result = total / final_den
    for t in range(4):
        out[t // 2, :, (t % 2) * 128 : (t % 2) * 128 + 128] = result[t * 8 : t * 8 + 8].astype(BF16)

    all_blocks.wait_send()
    all_sides.wait_send()
    for dz in FAR_FIRST:
        plane_wait(dz).wait_send()
        sib_copy(dz, core).wait_send()
    fresh_wait().wait_send()
    sib_fresh(core).wait_send()
    pair_copy.wait_send()
    for k in range(4):
        chunk_copy(k).wait_send()


def hand_over(result, rows, out, tail, sems):
    copies = [
        pltpu.make_async_copy(result, out, sems.at[0]),
        pltpu.make_async_copy(rows, tail, sems.at[1]),
    ]
    for copy in copies:
        copy.start()
    for copy in copies:
        copy.wait()


def per_device(kv_pool, queries, new_kv, lengths, block_dev, block_slot, owner_dev, owner_row):
    vmem = pl.BlockSpec(memory_space=pltpu.VMEM)
    dma = pltpu.SemaphoreType.DMA
    result, tail = pl.pallas_call(
        kernel,
        out_shape=(
            jax.ShapeDtypeStruct((2, 8, 256), BF16),
            jax.ShapeDtypeStruct((4, 2048), BF16),
        ),
        in_specs=[pl.BlockSpec(memory_space=pl.ANY)] + [vmem] * 6 + [pl.BlockSpec(memory_space=pltpu.SMEM)],
        out_specs=(vmem, vmem),
        scratch_shapes=[
            pltpu.VMEM((SLOTS, 128, 2048), BF16),
            pltpu.VMEM((2, 4, 16, 32, 128), BF16),
            pltpu.VMEM((2, CHIPS, 16, 128), BF16),
            pltpu.VMEM((2, 4, 512, 128), F32),
            pltpu.VMEM((2, 4, 128, 128), F32),
            pltpu.VMEM((SLOTS, 128, 128), BF16),
            pltpu.VMEM((SLOTS, 32, 128), F32),
            pltpu.VMEM((SLOTS, 128), F32),
            pltpu.VMEM((SLOTS, 128), F32),
            pltpu.VMEM((128, 128), F32),
            pltpu.VMEM((2, 2, REQS, 128), F32),
            pltpu.VMEM((2, REQS, 128), F32),
            pltpu.VMEM((REQS, 128), F32),
            pltpu.VMEM((128, 128), F32),
            pltpu.VMEM((128, 128), F32),
            pltpu.VMEM((2, 4, 512, 128), F32),
            pltpu.VMEM((4, 4, 128, 128), F32),
            pltpu.VMEM((CHIPS, 32, 128), BF16),
            pltpu.VMEM((CHIPS, 32, 128), BF16),
            pltpu.VMEM((CHIPS, 1, 128), F32),
            pltpu.VMEM((CHIPS, 1, 128), F32),
            pltpu.VMEM((64, 128), F32),
            pltpu.VMEM((40, 128), I32),
            pltpu.SMEM((40, 128), I32),
            pltpu.VMEM((40, 128), I32),
            dma((KV_PARTS,)),
            dma((KV_PARTS,)),
            dma((5,)),
            dma((5,)),
            dma((5,)),
            dma((5,)),
            dma((2,)),
            dma((4,)),
            dma((4,)),
            dma((4,)),
            dma,
        ],
        compiler_params=pltpu.CompilerParams(
            collective_id=0, has_side_effects=True, vmem_limit_bytes=56 * 1024 * 1024
        ),
    )(kv_pool, queries, new_kv, block_dev, block_slot, owner_dev, owner_row, lengths)
    anywhere = pl.BlockSpec(memory_space=pltpu.HBM)
    return pl.pallas_call(
        hand_over,
        out_shape=(
            jax.ShapeDtypeStruct((2, 8, 256), BF16),
            jax.ShapeDtypeStruct((4, 2048), BF16),
        ),
        in_specs=[anywhere] * 2,
        out_specs=(anywhere, anywhere),
        scratch_shapes=[dma((2,))],
    )(result, tail)


def solution(mesh):
    placed = (
        P(("inst", "seq"), None, None),
        P(None, "inst", "seq"),
        P(None, "inst", "seq"),
        P(),
        P(),
        P(),
        P(),
        P(),
    )
    return jax.shard_map(
        per_device,
        mesh=mesh,
        in_specs=placed,
        out_specs=(P(None, "inst", "seq"), P(("inst", "seq"), None)),
        check_vma=False,
    )
```

time: 50 us -> 50.3 us (level)
  Pallas kernels: 46.4 us -> 49.5 us
  local copies, waits for them, and re-layouts: 2.62 us -> 0 us
    unnamed x2 -> x0, local copies, waits for them, and re-layouts: 2.62 us -> none
    pallas_call x0 -> x1, Pallas kernels: none -> 1.87 us  [per_device(): pl.pallas_call(hand_over, out_shape=(jax.ShapeDtypeStruct((2, 8, 256), BF...]
    pallas_call x1, Pallas kernels: 46.4 us -> 47.7 us  [per_device(): pl.pallas_call(kernel, out_shape=(jax.ShapeDtypeStruct((2, 8, 256), BF16)...]
where the time goes in v2:
time: 50.3 us; the launch traced here: 50.2 us
  Pallas kernels  49.5 us (98%)
  between operations  0.64 us (1%)
    pallas_call x1, Pallas kernels, per_device(): pl.pallas_call(kernel, out_shape=(jax.ShapeDtypeStruct((2, 8, 256), BF16)...  47.7 us
    pallas_call x1, Pallas kernels, per_device(): pl.pallas_call(hand_over, out_shape=(jax.ShapeDtypeStruct((2, 8, 256), BF...  1.87 us

profile of v2, /device:TPU:1, one launch (start us, length us, event | category | flops | bytes accessed | tf_op | source)
XLA Modules:
  0.0 50.2 jit_solution(12531953183039777386)
XLA Ops:
  0.6 47.7 %shard_map.95 = (bf16[2,8,256]{2,1,0:T(8,128)(2,1)}, bf16[4,2048]{1,0:T(4,128)(2,1)}) custom-call(bf16[32,128,2048]{2,1,0:T(8,128)(2,1)} %kv.1, bf16[2,8,256]{2,1,0:T(8,128)(2,1)} %q.1, bf16[2,8,64]{2,1,0:T(8,128)(2,1)} %nk.1, s32[32,128]{1,0:T(8,128)} %dev.1, s32[32,128]{1,0:T(8,128)} %slot.1, s32[2,32]{1,0:T(2,128)} %own_dev.1, s32[2,32]{1,0:T(2,128)} %own_row.1, ...), custom_call_target="tpu_custom_call" | custom-call | tf_op jit(solution)/shard_map/pallas_call | solution.py:493
  48.3 1.9 %shard_map.96 = (bf16[2,8,256]{2,1,0:T(8,128)(2,1)}, bf16[4,2048]{1,0:T(4,128)(2,1)}) custom-call(bf16[2,8,256]{2,1,0:T(8,128)(2,1)} %get-tuple-element.4.result, bf16[4,2048]{1,0:T(4,128)(2,1)} %get-tuple-element.5.rows), custom_call_target="tpu_custom_call" | custom-call | tf_op jit(solution)/shard_map/pallas_call | solution.py:544

commit v3 on v2

--- a/solution.py
+++ b/solution.py
@@ -19,7 +19,7 @@
 LOW = -1e30
 SCALE = 1.0 / math.sqrt(128)
 UNROLL = 4
-GROUP = 8
+GROUP = 16
 KV_PARTS = SLOTS // UNROLL
 FAR_FIRST = (3, 2, 1, 0)
 
@@ -40,9 +40,10 @@
 
 
 def kernel(
-    kv, q, nk, dev, slot, own_dev, own_row, lens, out, tail,
+    kv, q_in, nk_in, dev_in, slot_in, own_dev_in, own_row_in, lens_in, out_at, tail_at,
+    q, nk, dev, slot, own_dev, own_row, lens, out, tail,
     kvb, gat, gnb, gq, gn, wb, cb, mb, db, fb, mx, lift, mc, mt, dt, s32, r32, sb, rb, ss, rs, tl, meta, smeta, codes,
-    k_sem, v_sem, sg, rg, s_sib, r_sib, m_sems, s_chunk, r_chunk, all_sems, meta_sem,
+    k_sem, v_sem, sg, rg, s_sib, r_sib, m_sems, s_chunk, r_chunk, all_sems, meta_sem, io_sem,
 ):
     z = lax.axis_index("inst")
     c = lax.axis_index("seq")
@@ -55,6 +56,16 @@
     def place(pz, py, px):
         return (pz, py * 8 + px * 2 + core)
 
+    loads = [
+        pltpu.make_async_copy(src, dst, io_sem.at[k])
+        for k, (src, dst) in enumerate([
+            (q_in, q), (nk_in, nk), (dev_in, dev), (slot_in, slot),
+            (own_dev_in, own_dev), (own_row_in, own_row), (lens_in, lens),
+        ])
+    ]
+    for load in loads:
+        load.start()
+
     def offset(d):
         return (z + d // 16) % 4, (y + (d // 4) % 4) % 4, (x + d % 4) % 4
 
@@ -81,6 +92,8 @@
         key_copy(part).start()
 
     spot = y * 4 + x
+    for load in loads[:2]:
+        load.wait()
     own = [q[s].astype(F32) for s in range(2)]
     gat[core, z, spot] = jnp.concatenate(
         [own[0][:, :128], own[0][:, 128:], own[1][:, :128], own[1][:, 128:]], axis=0
@@ -145,6 +158,8 @@
     def _(d):
         fresh_copy(d).start()
 
+    for load in loads[2:]:
+        load.wait()
     mine = jnp.where(dev[...] == me, slot[...], -1)
     code = iota((REQS, 128), 0) * 128 + iota((REQS, 128), 1) + 1
 
@@ -195,34 +210,43 @@
         sib_copy(dz, sib).wait_recv()
         widen(sib, dz)
 
-    token = iota((128, 128), 0)
-    head_of = iota((16, 128), 1) // 16
-    pick = [jnp.where(head_of == g, 1.0, 0.0).astype(BF16) for g in range(8)]
+    lane128 = iota((128, 128), 1)
+    blank = jnp.zeros((16, 128), BF16)
+    mt[...] = jnp.zeros((128, 128), F32)
+    dt[...] = jnp.zeros((128, 128), F32)
 
     @pl.loop(0, KV_PARTS)
     def _(part):
         key_copy(part).wait()
+        peaks = mt[...]
+        sums = dt[...]
         for e in range(UNROLL):
             n = part * UNROLL + e
             r = jnp.maximum(smeta[n, 0], 0)
             b = (jnp.maximum(smeta[n, 1], 1) - 1) % 128
             count = jnp.where(smeta[n, 1] > 0, lens[r] - b * 128, 0)
             parts = [gq[of, r // 8, pl.ds(r % 8, 64, stride=8), :].reshape(8, 8, 128) for of in range(2)]
-            turned = jnp.concatenate(parts, axis=1).reshape(128, 128).T.astype(BF16).reshape(8, 16, 128)
-            score = jnp.zeros((128, 128), F32)
+            heads = jnp.concatenate(parts, axis=1).astype(BF16)
+            score = []
             for kt in range(4):
-                pair = [(turned * pick[g]).reshape(128, 128) for g in (2 * kt, 2 * kt + 1)]
-                score = score + jnp.dot(
-                    kvb[n, :, kt * 256 : kt * 256 + 256], jnp.concatenate(pair, axis=0),
-                    preferred_element_type=F32,
-                )
-            valid = token < count
-            score = jnp.where(valid, score * SCALE, LOW)
-            peak = jnp.max(score, axis=0, keepdims=True)
+                first = jnp.concatenate([heads[2 * kt], blank], axis=1)
+                second = jnp.concatenate([blank, heads[2 * kt + 1]], axis=1)
+                score.append(lax.dot_general(
+                    jnp.concatenate([first, second], axis=0), kvb[n, :, kt * 256 : kt * 256 + 256],
+                    (((1,), (1,)), ((), ())), preferred_element_type=F32,
+                ))
+            valid = lane128 < count
+            score = jnp.where(valid, jnp.concatenate(score, axis=0) * SCALE, LOW)
+            peak = jnp.max(score, axis=1, keepdims=True)
             w = jnp.where(valid, jnp.exp(score - peak), 0.0).astype(BF16)
-            mb[pl.ds(n, 1), :] = peak
-            db[pl.ds(n, 1), :] = jnp.sum(w.astype(F32), axis=0, keepdims=True)
-            wb[n] = w.T
+            wb[n] = w
+            peaks = jnp.where(lane128 == n, peak, peaks)
+            sums = jnp.where(lane128 == n, jnp.sum(w.astype(F32), axis=1, keepdims=True), sums)
+        mt[...] = peaks
+        dt[...] = sums
+
+    mb[...] = mt[...].T[:SLOTS]
+    db[...] = dt[...].T[:SLOTS]
 
     fresh_wait().wait_recv()
     sib_fresh(core).start()
@@ -464,6 +488,13 @@
     for t in range(4):
         out[t // 2, :, (t % 2) * 128 : (t % 2) * 128 + 128] = result[t * 8 : t * 8 + 8].astype(BF16)
 
+    stores = [
+        pltpu.make_async_copy(src, dst, io_sem.at[k])
+        for k, (src, dst) in enumerate([(out, out_at), (tail, tail_at)])
+    ]
+    for store in stores:
+        store.start()
+
     all_blocks.wait_send()
     all_sides.wait_send()
     for dz in FAR_FIRST:
@@ -474,6 +505,8 @@
     pair_copy.wait_send()
     for k in range(4):
         chunk_copy(k).wait_send()
+    for store in stores:
+        store.wait()
 
 
 def hand_over(result, rows, out, tail, sems):
@@ -488,7 +521,7 @@
 
 
 def per_device(kv_pool, queries, new_kv, lengths, block_dev, block_slot, owner_dev, owner_row):
-    vmem = pl.BlockSpec(memory_space=pltpu.VMEM)
+    anywhere = pl.BlockSpec(memory_space=pltpu.HBM)
     dma = pltpu.SemaphoreType.DMA
     result, tail = pl.pallas_call(
         kernel,
@@ -496,9 +529,18 @@
             jax.ShapeDtypeStruct((2, 8, 256), BF16),
             jax.ShapeDtypeStruct((4, 2048), BF16),
         ),
-        in_specs=[pl.BlockSpec(memory_space=pl.ANY)] + [vmem] * 6 + [pl.BlockSpec(memory_space=pltpu.SMEM)],
-        out_specs=(vmem, vmem),
+        in_specs=[anywhere] * 8,
+        out_specs=(anywhere, anywhere),
         scratch_shapes=[
+            pltpu.VMEM((2, 8, 256), BF16),
+            pltpu.VMEM((2, 8, 64), BF16),
+            pltpu.VMEM((REQS, 128), I32),
+            pltpu.VMEM((REQS, 128), I32),
+            pltpu.VMEM((2, REQS), I32),
+            pltpu.VMEM((2, REQS), I32),
+            pltpu.SMEM((REQS,), I32),
+            pltpu.VMEM((2, 8, 256), BF16),
+            pltpu.VMEM((4, 2048), BF16),
             pltpu.VMEM((SLOTS, 128, 2048), BF16),
             pltpu.VMEM((2, 4, 16, 32, 128), BF16),
             pltpu.VMEM((2, CHIPS, 16, 128), BF16),
@@ -535,12 +577,12 @@
             dma((4,)),
             dma((4,)),
             dma,
+            dma((7,)),
         ],
         compiler_params=pltpu.CompilerParams(
             collective_id=0, has_side_effects=True, vmem_limit_bytes=56 * 1024 * 1024
         ),
     )(kv_pool, queries, new_kv, block_dev, block_slot, owner_dev, owner_row, lengths)
-    anywhere = pl.BlockSpec(memory_space=pltpu.HBM)
     return pl.pallas_call(
         hand_over,
         out_shape=(

time: 50.3 us -> 48.5 us (0.964)
  Pallas kernels: 49.5 us -> 47.7 us
    pallas_call x1, Pallas kernels: 47.7 us -> 45.9 us  [per_device(): pl.pallas_call(kernel, out_shape=(jax.ShapeDtypeStruct((2, 8, 256), BF16)...]
where the time goes in v3:
time: 48.5 us; the launch traced here: 48.4 us
  Pallas kernels  47.7 us (98%)
  between operations  0.64 us (1%)
    pallas_call x1, Pallas kernels, per_device(): pl.pallas_call(kernel, out_shape=(jax.ShapeDtypeStruct((2, 8, 256), BF16)...  45.9 us
    pallas_call x1, Pallas kernels, per_device(): pl.pallas_call(hand_over, out_shape=(jax.ShapeDtypeStruct((2, 8, 256), BF...  1.87 us

profile of v3, /device:TPU:1, one launch (start us, length us, event | category | flops | bytes accessed | tf_op | source)
XLA Modules:
  0.0 48.4 jit_solution(13884872399254023630)
XLA Ops:
  0.6 45.9 %shard_map.95 = (bf16[2,8,256]{2,1,0:T(8,128)(2,1)}, bf16[4,2048]{1,0:T(4,128)(2,1)}) custom-call(bf16[32,128,2048]{2,1,0:T(8,128)(2,1)} %kv.1, bf16[2,8,256]{2,1,0:T(8,128)(2,1)} %q_in.1, bf16[2,8,64]{2,1,0:T(8,128)(2,1)} %nk_in.1, s32[32,128]{1,0:T(8,128)} %dev_in.1, s32[32,128]{1,0:T(8,128)} %slot_in.1, s32[2,32]{1,0:T(2,128)} %own_dev_in.1, ...), custom_call_target="tpu_custom_call" | custom-call | tf_op jit(solution)/shard_map/pallas_call | solution.py:526
  46.5 1.9 %shard_map.96 = (bf16[2,8,256]{2,1,0:T(8,128)(2,1)}, bf16[4,2048]{1,0:T(4,128)(2,1)}) custom-call(bf16[2,8,256]{2,1,0:T(8,128)(2,1)} %get-tuple-element.4.result, bf16[4,2048]{1,0:T(4,128)(2,1)} %get-tuple-element.5.rows), custom_call_target="tpu_custom_call" | custom-call | tf_op jit(solution)/shard_map/pallas_call | solution.py:586

commit v4 on v3

v4 whole, which is shorter than its diff:
```python
import math

import jax
import jax.numpy as jnp
from jax import lax
from jax.experimental import pallas as pl
from jax.experimental.pallas import tpu as pltpu
from jax.sharding import PartitionSpec as P

MESH = pl.DeviceIdType.MESH
F32 = jnp.float32
BF16 = jnp.bfloat16
I32 = jnp.int32

N = 4
CHIPS = 64
SLOTS = 32
REQS = 32
LOW = -1e30
SCALE = 1.0 / math.sqrt(128)
UNROLL = 4
GROUP = 16
KV_PARTS = SLOTS // UNROLL


def iota(shape, dim):
    return lax.broadcasted_iota(I32, shape, dim)


def halves(first, second, late):
    lane = iota(first.shape, 1)
    if late is True:
        return jnp.where(lane < 64, pltpu.roll(first, 64, 1), second)
    if late is False:
        return jnp.where(lane < 64, first, pltpu.roll(second, 64, 1))
    low = jnp.where(late, pltpu.roll(first, 64, 1), first)
    high = jnp.where(late, second, pltpu.roll(second, 64, 1))
    return jnp.where(lane < 64, low, high)


def kernel(
    kv, q_in, nk_in, dev_in, slot_in, own_dev_in, own_row_in, lens_in, out_at, tail_at,
    q, nk, dev, slot, own_dev, own_row, lens, out, tail,
    kvb, gat, nx, tile, gnt, gq, gn, wb, pk, dn, cb, mx, mxr, mt, uw, s32, r32, sb, rb, ss, rs, tl, meta, smeta, codes,
    k_sem, v_sem, sg, rg, s_sib, r_sib, n_sems, s_m, r_m, s_chunk, r_chunk, all_sems, meta_sem, io_sem,
):
    z = lax.axis_index("inst")
    c = lax.axis_index("seq")
    y, x, core = c // 8, (c // 2) % 4, c % 2
    me = z * 32 + c
    chip = z * 16 + y * 4 + x
    sib = 1 - core
    sibling = (z, y * 8 + x * 2 + sib)

    def place(pz, py, px):
        return (pz, py * 8 + px * 2 + core)

    loads = [
        pltpu.make_async_copy(src, dst, io_sem.at[k])
        for k, (src, dst) in enumerate([
            (q_in, q), (nk_in, nk), (dev_in, dev), (slot_in, slot),
            (own_dev_in, own_dev), (own_row_in, own_row), (lens_in, lens),
        ])
    ]
    for load in loads:
        load.start()

    def offset(d):
        return (z + d // 16) % 4, (y + (d // 4) % 4) % 4, (x + d % 4) % 4

    barrier = pltpu.get_barrier_semaphore()

    @pl.loop(1, CHIPS)
    def _(d):
        pl.semaphore_signal(barrier, inc=1, device_id=place(*offset(d)), device_id_type=MESH)

    pl.semaphore_signal(barrier, inc=1, device_id=sibling, device_id_type=MESH)

    def key_copy(part):
        span = pl.ds(part * UNROLL, UNROLL)
        cols = pl.ds(0, 1024)
        return pltpu.make_async_copy(kv.at[span, :, cols], kvb.at[span, :, cols], k_sem.at[part])

    def value_copy(part):
        span = pl.ds(part * UNROLL, UNROLL)
        cols = pl.ds(1024, 1024)
        return pltpu.make_async_copy(kv.at[span, :, cols], kvb.at[span, :, cols], v_sem.at[part])

    @pl.loop(0, KV_PARTS)
    def _(part):
        key_copy(part).start()

    spot = z * 4 + x
    for load in loads[:2]:
        load.wait()
    own = [q[s].astype(F32) for s in range(2)]
    gat[core, y, spot] = jnp.concatenate(
        [own[0][:, :128], own[0][:, 128:], own[1][:, :128], own[1][:, 128:]], axis=0
    ).astype(BF16)
    nx[0] = jnp.concatenate([nk[0].astype(F32), nk[1].astype(F32)], axis=1)

    pl.semaphore_wait(barrier, CHIPS)

    def turn(k):
        return (y + k) % 4

    def beside(e, py):
        return (z + e // 4) % 4, py, (x + e % 4) % 4

    def query_copy(k, e):
        block = gat.at[core, y, spot]
        return pltpu.make_async_remote_copy(
            src_ref=block, dst_ref=block, send_sem=sg.at[k], recv_sem=rg.at[k],
            device_id=place(*beside(e, (y + 4 - k) % 4)), device_id_type=MESH,
        )

    def plane_wait(k, blocks=16):
        block = gat.at[core, turn(k), pl.ds(0, blocks)]
        return pltpu.make_async_remote_copy(
            src_ref=block, dst_ref=block, send_sem=sg.at[k], recv_sem=rg.at[k],
            device_id=sibling, device_id_type=MESH,
        )

    def sib_copy(k, of):
        block = gat.at[of, turn(k)]
        return pltpu.make_async_remote_copy(
            src_ref=block, dst_ref=block, send_sem=s_sib.at[k], recv_sem=r_sib.at[k],
            device_id=sibling, device_id_type=MESH,
        )

    @pl.loop(1, CHIPS)
    def _(d):
        query_copy(d // 16, d % 16).start()

    pair_rows = pltpu.make_async_remote_copy(
        src_ref=nx.at[0], dst_ref=nx.at[1], send_sem=n_sems.at[0], recv_sem=n_sems.at[1],
        device_id=sibling, device_id_type=MESH,
    )
    pair_rows.start()
    shelf = z * 8 + y * 2 + x // 2

    def fresh_copy(d):
        return pltpu.make_async_remote_copy(
            src_ref=tile, dst_ref=gnt.at[x % 2, shelf], send_sem=n_sems.at[2], recv_sem=n_sems.at[3],
            device_id=place(*offset(d)), device_id_type=MESH,
        )

    def fresh_wait(blocks):
        block = gnt.at[0, pl.ds(0, blocks)]
        return pltpu.make_async_remote_copy(
            src_ref=block, dst_ref=block, send_sem=n_sems.at[2], recv_sem=n_sems.at[3],
            device_id=sibling, device_id_type=MESH,
        )

    def sib_fresh(of):
        block = gnt.at[(x + of) % 2]
        return pltpu.make_async_remote_copy(
            src_ref=block, dst_ref=block, send_sem=n_sems.at[4], recv_sem=n_sems.at[5],
            device_id=sibling, device_id_type=MESH,
        )

    @pl.loop(0, KV_PARTS)
    def _(part):
        value_copy(part).start()

    for load in loads[2:]:
        load.wait()
    mine = jnp.where(dev[...] == me, slot[...], -1)
    code = iota((REQS, 128), 0) * 128 + iota((REQS, 128), 1) + 1

    @pl.loop(0, SLOTS // 4)
    def _(group):
        for e in range(4):
            n = group * 4 + e
            codes[pl.ds(n, 1), :] = jnp.sum(jnp.where(mine == n, code, 0), axis=0, keepdims=True)

    owned = jnp.where(own_dev[...] == me, own_row[...], -1)
    row_code = iota((2, REQS), 0) * REQS + iota((2, REQS), 1) + 1
    pad_row = jnp.zeros((1, 96), I32)
    for e in range(4):
        hit = jnp.sum(jnp.where(owned == e, row_code, 0), axis=0, keepdims=True)
        codes[SLOTS + e : SLOTS + e + 1, :] = jnp.concatenate([hit, pad_row], axis=1)
    codes[SLOTS + 4 :, :] = jnp.zeros((4, 128), I32)

    found = jnp.broadcast_to(jnp.sum(codes[...], axis=1, keepdims=True), (40, 128))
    held = found[:SLOTS]
    req_col = jnp.where(held > 0, jnp.minimum((held - 1) >> 7, REQS - 1), -1)
    rows, lanes = iota((SLOTS, 128), 0), iota((SLOTS, 128), 1)
    req_row = jnp.sum(jnp.where(rows == lanes, req_col, 0), axis=0, keepdims=True)
    req_row = jnp.where(lanes < SLOTS, jnp.broadcast_to(req_row, (SLOTS, 128)), -2)
    before = jnp.max(jnp.where((req_row == req_col) & (lanes < rows), lanes, -1), axis=1, keepdims=True)
    last = jnp.max(jnp.where(req_row == rows, lanes, -1), axis=1, keepdims=True)
    meta[:SLOTS] = jnp.where(
        lanes == 0, req_col, jnp.where(lanes == 1, held, jnp.where(lanes == 2, before, last))
    )
    meta[SLOTS:] = found[SLOTS:]
    meta_copy = pltpu.make_async_copy(meta, smeta, meta_sem)
    meta_copy.start()

    pair_rows.wait_recv()
    both_rows = [jnp.where(core == of, nx[0], nx[1]) for of in range(2)]
    tile[...] = jnp.concatenate(both_rows, axis=0).astype(BF16)

    @pl.when(core == 0)
    def _():
        gnt[x % 2, shelf] = tile[...]

    @pl.loop(0, 32)
    def _(half):
        @pl.when(2 * half + core > 0)
        def _():
            fresh_copy(2 * half + core).start()

    plane_wait(0, 15).wait_recv()
    sib_copy(0, core).start()
    meta_copy.wait()

    @pl.loop(0, KV_PARTS)
    def _(part):
        key_copy(part).wait()

    lanes = iota((32, 128), 1)
    blank = jnp.zeros((16, 128), BF16)

    def chunk_copy(k):
        return pltpu.make_async_remote_copy(
            src_ref=s32.at[k, sib], dst_ref=r32.at[k],
            send_sem=s_chunk.at[k], recv_sem=r_chunk.at[k], device_id=sibling, device_id_type=MESH,
        )

    def peak_copy(k):
        return pltpu.make_async_remote_copy(
            src_ref=mx.at[k], dst_ref=mxr.at[k], send_sem=s_m.at[k], recv_sem=r_m.at[k],
            device_id=sibling, device_id_type=MESH,
        )

    def block_copy(to_chip, to):
        return pltpu.make_async_remote_copy(
            src_ref=sb.at[to_chip], dst_ref=rb.at[chip], send_sem=all_sems.at[0], recv_sem=all_sems.at[1],
            device_id=to, device_id_type=MESH,
        )

    def side_copy(to_chip, to):
        return pltpu.make_async_remote_copy(
            src_ref=ss.at[to_chip], dst_ref=rs.at[chip], send_sem=all_sems.at[2], recv_sem=all_sems.at[3],
            device_id=to, device_id_type=MESH,
        )

    def scores(k):
        cols = pl.ds(pl.multiple_of(turn(k) * 256, 256), 256)

        @pl.loop(0, SLOTS // GROUP, init_carry=jnp.full((32, 128), LOW, F32))
        def most(group, most):
            for e in range(GROUP):
                n = group * GROUP + e
                r = jnp.maximum(smeta[n, 0], 0)
                b = (jnp.maximum(smeta[n, 1], 1) - 1) % 128
                count = jnp.where(smeta[n, 1] > 0, lens[r] - b * 128, 0)
                parts = [gq[of, r // 8, pl.ds(r % 8, 16, stride=8), :].reshape(2, 8, 128) for of in range(2)]
                heads = jnp.concatenate(parts, axis=1).astype(BF16)
                first = jnp.concatenate([heads[0], blank], axis=1)
                second = jnp.concatenate([blank, heads[1]], axis=1)
                score = lax.dot_general(
                    jnp.concatenate([first, second], axis=0), kvb[n, :, cols],
                    (((1,), (1,)), ((), ())), preferred_element_type=F32,
                )
                valid = lanes < count
                score = jnp.where(valid, score * SCALE, LOW)
                peak = jnp.max(score, axis=1, keepdims=True)
                w = jnp.where(valid, jnp.exp(score - peak), 0.0).astype(BF16)
                wb[n] = w
                pk[n] = jnp.broadcast_to(peak, (32, 128))
                dn[n] = jnp.broadcast_to(jnp.sum(w.astype(F32), axis=1, keepdims=True), (32, 128))
                most = jnp.where(lanes == smeta[n, 0], jnp.maximum(most, peak), most)
            return most

        return most

    def values(k, most):
        cols = pl.ds(pl.multiple_of(1024 + turn(k) * 256, 256), 256)

        @pl.loop(0, SLOTS // GROUP, init_carry=jnp.zeros((32, 128), F32))
        def den(group, den):
            for e in range(GROUP):
                n = group * GROUP + e
                r = smeta[n, 0]
                best = jnp.max(jnp.where(lanes == r, most, LOW), axis=1, keepdims=True)
                factor = jnp.exp(pk[n] - best)
                both = jnp.dot(wb[n], kvb[n, :, cols], preferred_element_type=F32)
                num = jnp.concatenate([both[:16, :128], both[16:, 128:]], axis=0)
                prev = smeta[n, 2]
                earlier = jnp.where(prev >= 0, cb[jnp.maximum(prev, 0)], 0.0)
                cb[n] = num * factor + earlier
                den = den + jnp.where(lanes == r, factor * dn[n], 0.0)
            return den

        mx[k, 0] = most
        mx[k, 1] = den
        peak_copy(k).start()

    def hand_on(k):
        @pl.loop(0, 4)
        def _(i):
            for rl in range(8):
                end = smeta[i * 8 + rl, 3]
                sums = jnp.where(end >= 0, cb[jnp.maximum(end, 0)], 0.0)
                for xh in range(2):
                    for of in range(2):
                        at = pl.ds(xh * 64 + rl, 8, stride=8)
                        s32[k, of, i, at, :] = sums[xh * 16 + of * 8 : xh * 16 + of * 8 + 8]

        chunk_copy(k).start()

    def merge(k):
        kt = turn(k)
        peak_copy(k).wait_recv()
        top, other = mx[k, 0], mxr[k, 0]
        chip_top = jnp.maximum(top, other)
        mine_f, other_f = jnp.exp(top - chip_top), jnp.exp(other - chip_top)
        chip_den = mx[k, 1] * mine_f + mxr[k, 1] * other_f
        mt[...] = jnp.concatenate([mine_f, other_f, chip_top, chip_den], axis=0)
        for w in range(2):
            for xh in range(2):
                row = pl.multiple_of(64 + w * 32 + xh * 16 + core * 8, 8)
                uw[w * 16 + xh * 8 : w * 16 + xh * 8 + 8, :] = mt[pl.ds(row, 8), :]
        lane4 = iota((4, 128), 1)
        packed = [jnp.zeros((4, 128), F32) for _ in range(4)]
        for w in range(2):
            for t in range(4):
                got = uw[pl.ds(w * 16 + t, 4, stride=4), :]
                to = w * 32 + t * 8
                for i in range(4):
                    there = pltpu.roll(got, (to - 8 * i) % 128, 1)
                    packed[i] = jnp.where((lane4 >= to) & (lane4 < to + 8), there, packed[i])
        for i in range(4):
            for j in range(4):
                ss[i * 16 + kt * 4 + j] = packed[i][j : j + 1, :]
        mt[...] = pltpu.roll(mt[...].T, (128 - core * 8) % 128, 1)
        chunk_copy(k).wait_recv()

        @pl.loop(0, 4)
        def _(i):
            factors = mt[pl.ds(pl.multiple_of(i * 8, 8), 8), :]
            for j in range(4):
                total = []
                for t in range(4):
                    lane = (j // 2) * 16 + (j % 2) * 4 + t
                    at = slice(j * 32 + t * 8, j * 32 + t * 8 + 8)
                    total.append(
                        s32[k, core, i, at, :] * factors[:, lane : lane + 1]
                        + r32[k, i, at, :] * factors[:, 32 + lane : 33 + lane]
                    )
                sb[i * 16 + kt * 4 + j] = jnp.concatenate(total, axis=0).astype(BF16)

    def send(k):
        kt = turn(k)

        @pl.loop(0, 16)
        def _(e):
            pz, _, px = beside(e, kt)
            to_chip, to = pz * 16 + kt * 4 + px, place(pz, kt, px)

            @pl.when(k * 16 + e > 0)
            def _():
                block_copy(to_chip, to).start()
                side_copy(to_chip, to).start()

    @pl.loop(0, 5)
    def _(k):
        @pl.when(k < 4)
        def _():
            sib_copy(k, sib).wait_recv()

            @pl.loop(0, 8)
            def _(part):
                of, i = part // 4, part % 4
                for j in range(4):
                    gq[of, i, j * 32 : j * 32 + 32, :] = gat[of, turn(k), i * 4 + j].astype(F32)

            most = scores(k)

            @pl.when(k < 3)
            def _():
                plane_wait(k + 1).wait_recv()
                sib_copy(k + 1, core).start()

            @pl.when(k == 0)
            def _():
                @pl.loop(0, KV_PARTS)
                def _(part):
                    value_copy(part).wait()

            values(k, most)

        @pl.when(k > 0)
        def _():
            merge(k - 1)
            send(k - 1)

        @pl.when(k < 4)
        def _():
            hand_on(k)

    rb[chip] = sb[chip]
    rs[chip] = ss[chip]

    @pl.when(core == 0)
    def _():
        fresh_wait(31).wait_recv()

    @pl.when(core == 1)
    def _():
        fresh_wait(32).wait_recv()

    sib_fresh(core).start()
    sib_fresh(sib).wait_recv()

    @pl.loop(0, 4)
    def _(i):
        for j in range(16):
            fresh = gnt[j % 2, i * 8 + j // 2].astype(F32)
            for of in range(2):
                gn[of, i, j * 8 : j * 8 + 8, :] = fresh[of * 8 : of * 8 + 8]

    @pl.loop(0, 4)
    def _(e):
        found_row = smeta[SLOTS + e, 0]
        which = jnp.maximum(found_row - 1, 0)
        late, r = which // 32, which % 32
        pair = [gn[of, r // 8, pl.ds(r % 8, 16, stride=8), :] for of in range(2)]
        tl[pl.ds(pl.multiple_of(e * 16, 16), 16), :] = jnp.where(found_row > 0, halves(pair[0], pair[1], late > 0), 0.0)
    for j in range(16):
        tail[:, j * 128 : j * 128 + 128] = tl[pl.ds(j, 4, stride=16), :].astype(BF16)

    head = y * 2 + x // 2
    new_rows = []
    for at in (head, head + 8):
        pair = [gn[of, z, pl.ds(pl.multiple_of(at * 8, 8), 8), :] for of in range(2)]
        new_rows.append([halves(pair[0], pair[1], late) for late in (False, True)])
    new_m, new_den, new_num = [], [], []
    for t in range(4):
        mine_q = q[t // 2].astype(F32)[:, (t % 2) * 128 : (t % 2) * 128 + 128]
        found_scores = [
            jnp.sum(mine_q * new_rows[0][j], axis=1, keepdims=True) * SCALE for j in range(t // 2 + 1)
        ]
        peak = found_scores[0]
        for more in found_scores[1:]:
            peak = jnp.maximum(peak, more)
        ws = [jnp.exp(v - peak).astype(BF16).astype(F32) for v in found_scores]
        new_m.append(peak)
        new_den.append(sum(ws[1:], ws[0]))
        num = ws[0] * new_rows[1][0]
        for j in range(1, len(ws)):
            num = num + ws[j] * new_rows[1][j]
        new_num.append(num)
    new_m = jnp.concatenate(new_m, axis=0)
    new_den = jnp.concatenate(new_den, axis=0)
    new_num = jnp.concatenate(new_num, axis=0)

    most = pl.ds(0, CHIPS - 1)
    all_blocks = pltpu.make_async_remote_copy(
        src_ref=sb.at[most], dst_ref=rb.at[most], send_sem=all_sems.at[0], recv_sem=all_sems.at[1],
        device_id=sibling, device_id_type=MESH,
    )
    all_sides = pltpu.make_async_remote_copy(
        src_ref=ss.at[most], dst_ref=rs.at[most], send_sem=all_sems.at[2], recv_sem=all_sems.at[3],
        device_id=sibling, device_id_type=MESH,
    )
    all_sides.wait_recv()
    side = rs[...].reshape(CHIPS, 128)
    side = jnp.concatenate([side, jnp.zeros((128 - CHIPS, 128), F32)], axis=0).T
    side_m, side_den = side[0:32, :CHIPS], side[32:64, :CHIPS]
    final_m = jnp.maximum(jnp.max(side_m, axis=1, keepdims=True), new_m)
    scales = jnp.exp(side_m - final_m)
    new_scale = jnp.exp(new_m - final_m)
    final_den = jnp.sum(scales * side_den, axis=1, keepdims=True) + new_den * new_scale
    total = new_num * new_scale
    all_blocks.wait_recv()
    scales = jnp.concatenate([scales, jnp.zeros((32, 128 - CHIPS), F32)], axis=1)

    @pl.loop(0, CHIPS // 8, init_carry=(total, scales))
    def total_and_scales(group, carry):
        total, scales = carry
        for e in range(8):
            total = total + scales[:, e : e + 1] * rb[group * 8 + e].astype(F32)
        return total, pltpu.roll(scales, 120, 1)

    total = total_and_scales[0]
    result = total / final_den
    for t in range(4):
        out[t // 2, :, (t % 2) * 128 : (t % 2) * 128 + 128] = result[t * 8 : t * 8 + 8].astype(BF16)

    stores = [
        pltpu.make_async_copy(src, dst, io_sem.at[k])
        for k, (src, dst) in enumerate([(out, out_at), (tail, tail_at)])
    ]
    for store in stores:
        store.start()

    all_blocks.wait_send()
    all_sides.wait_send()
    plane_wait(0, 15).wait_send()
    for k in range(1, 4):
        plane_wait(k).wait_send()
    for k in range(4):
        sib_copy(k, core).wait_send()
        peak_copy(k).wait_send()
        chunk_copy(k).wait_send()
    pair_rows.wait_send()

    @pl.when(core == 0)
    def _():
        fresh_wait(31).wait_send()

    @pl.when(core == 1)
    def _():
        fresh_wait(32).wait_send()

    sib_fresh(core).wait_send()
    for store in stores:
        store.wait()


def hand_over(result, rows, out, tail, sems):
    copies = [
        pltpu.make_async_copy(result, out, sems.at[0]),
        pltpu.make_async_copy(rows, tail, sems.at[1]),
    ]
    for copy in copies:
        copy.start()
    for copy in copies:
        copy.wait()


def per_device(kv_pool, queries, new_kv, lengths, block_dev, block_slot, owner_dev, owner_row):
    anywhere = pl.BlockSpec(memory_space=pltpu.HBM)
    dma = pltpu.SemaphoreType.DMA
    result, tail = pl.pallas_call(
        kernel,
        out_shape=(
            jax.ShapeDtypeStruct((2, 8, 256), BF16),
            jax.ShapeDtypeStruct((4, 2048), BF16),
        ),
        in_specs=[anywhere] * 8,
        out_specs=(anywhere, anywhere),
        scratch_shapes=[
            pltpu.VMEM((2, 8, 256), BF16),
            pltpu.VMEM((2, 8, 64), BF16),
            pltpu.VMEM((REQS, 128), I32),
            pltpu.VMEM((REQS, 128), I32),
            pltpu.VMEM((2, REQS), I32),
            pltpu.VMEM((2, REQS), I32),
            pltpu.SMEM((REQS,), I32),
            pltpu.VMEM((2, 8, 256), BF16),
            pltpu.VMEM((4, 2048), BF16),
            pltpu.VMEM((SLOTS, 128, 2048), BF16),
            pltpu.VMEM((2, 4, 16, 32, 128), BF16),
            pltpu.VMEM((2, 8, 128), F32),
            pltpu.VMEM((16, 128), BF16),
            pltpu.VMEM((2, 32, 16, 128), BF16),
            pltpu.VMEM((2, 4, 128, 128), F32),
            pltpu.VMEM((2, 4, 128, 128), F32),
            pltpu.VMEM((SLOTS, 32, 128), BF16),
            pltpu.VMEM((SLOTS, 32, 128), F32),
            pltpu.VMEM((SLOTS, 32, 128), F32),
            pltpu.VMEM((SLOTS, 32, 128), F32),
            pltpu.VMEM((4, 2, 32, 128), F32),
            pltpu.VMEM((4, 2, 32, 128), F32),
            pltpu.VMEM((128, 128), F32),
            pltpu.VMEM((32, 128), F32),
            pltpu.VMEM((4, 2, 4, 128, 128), F32),
            pltpu.VMEM((4, 4, 128, 128), F32),
            pltpu.VMEM((CHIPS, 32, 128), BF16),
            pltpu.VMEM((CHIPS, 32, 128), BF16),
            pltpu.VMEM((CHIPS, 1, 128), F32),
            pltpu.VMEM((CHIPS, 1, 128), F32),
            pltpu.VMEM((64, 128), F32),
            pltpu.VMEM((40, 128), I32),
            pltpu.SMEM((40, 128), I32),
            pltpu.VMEM((40, 128), I32),
            dma((KV_PARTS,)),
            dma((KV_PARTS,)),
            dma((4,)),
            dma((4,)),
            dma((4,)),
            dma((4,)),
            dma((6,)),
            dma((4,)),
            dma((4,)),
            dma((4,)),
            dma((4,)),
            dma((4,)),
            dma,
            dma((7,)),
        ],
        compiler_params=pltpu.CompilerParams(
            collective_id=0, has_side_effects=True, vmem_limit_bytes=56 * 1024 * 1024
        ),
    )(kv_pool, queries, new_kv, block_dev, block_slot, owner_dev, owner_row, lengths)
    return pl.pallas_call(
        hand_over,
        out_shape=(
            jax.ShapeDtypeStruct((2, 8, 256), BF16),
            jax.ShapeDtypeStruct((4, 2048), BF16),
        ),
        in_specs=[anywhere] * 2,
        out_specs=(anywhere, anywhere),
        scratch_shapes=[dma((2,))],
    )(result, tail)


def solution(mesh):
    placed = (
        P(("inst", "seq"), None, None),
        P(None, "inst", "seq"),
        P(None, "inst", "seq"),
        P(),
        P(),
        P(),
        P(),
        P(),
    )
    return jax.shard_map(
        per_device,
        mesh=mesh,
        in_specs=placed,
        out_specs=(P(None, "inst", "seq"), P(("inst", "seq"), None)),
        check_vma=False,
    )
```

time: 48.5 us -> 43.8 us (0.903)
  Pallas kernels: 47.7 us -> 43.1 us
    pallas_call x1, Pallas kernels: 45.9 us -> 41.2 us  [per_device(): pl.pallas_call(kernel, out_shape=(jax.ShapeDtypeStruct((2, 8, 256), BF16)...]
where the time goes in v4:
time: 43.8 us; the launch traced here: 43.7 us
  Pallas kernels  43.1 us (98%)
  between operations  0.64 us (1%)
    pallas_call x1, Pallas kernels, per_device(): pl.pallas_call(kernel, out_shape=(jax.ShapeDtypeStruct((2, 8, 256), BF16)...  41.2 us
    pallas_call x1, Pallas kernels, per_device(): pl.pallas_call(hand_over, out_shape=(jax.ShapeDtypeStruct((2, 8, 256), BF...  1.87 us

profile of v4, /device:TPU:1, one launch (start us, length us, event | category | flops | bytes accessed | tf_op | source)
XLA Modules:
  0.0 43.7 jit_solution(3052453281639755068)
XLA Ops:
  0.6 41.2 %shard_map.95 = (bf16[2,8,256]{2,1,0:T(8,128)(2,1)}, bf16[4,2048]{1,0:T(4,128)(2,1)}) custom-call(bf16[32,128,2048]{2,1,0:T(8,128)(2,1)} %kv.1, bf16[2,8,256]{2,1,0:T(8,128)(2,1)} %q_in.1, bf16[2,8,64]{2,1,0:T(8,128)(2,1)} %nk_in.1, s32[32,128]{1,0:T(8,128)} %dev_in.1, s32[32,128]{1,0:T(8,128)} %slot_in.1, s32[2,32]{1,0:T(2,128)} %own_dev_in.1, ...), custom_call_target="tpu_custom_call" | custom-call | tf_op jit(solution)/shard_map/pallas_call | solution.py:538
  41.8 1.9 %shard_map.96 = (bf16[2,8,256]{2,1,0:T(8,128)(2,1)}, bf16[4,2048]{1,0:T(4,128)(2,1)}) custom-call(bf16[2,8,256]{2,1,0:T(8,128)(2,1)} %get-tuple-element.4.result, bf16[4,2048]{1,0:T(4,128)(2,1)} %get-tuple-element.5.rows), custom_call_target="tpu_custom_call" | custom-call | tf_op jit(solution)/shard_map/pallas_call | solution.py:600

commit v5 on v4

--- a/solution.py
+++ b/solution.py
@@ -19,7 +19,8 @@
 LOW = -1e30
 SCALE = 1.0 / math.sqrt(128)
 UNROLL = 4
-GROUP = 16
+GROUP = 32
+SHIFT = (0, 2, 1, 3)
 KV_PARTS = SLOTS // UNROLL
 
 
@@ -42,7 +43,7 @@
     kv, q_in, nk_in, dev_in, slot_in, own_dev_in, own_row_in, lens_in, out_at, tail_at,
     q, nk, dev, slot, own_dev, own_row, lens, out, tail,
     kvb, gat, nx, tile, gnt, gq, gn, wb, pk, dn, cb, mx, mxr, mt, uw, s32, r32, sb, rb, ss, rs, tl, meta, smeta, codes,
-    k_sem, v_sem, sg, rg, s_sib, r_sib, n_sems, s_m, r_m, s_chunk, r_chunk, all_sems, meta_sem, io_sem,
+    k_sem, v_sem, sg, rg, s_sib, r_sib, n_sems, s_m, r_m, s_chunk, r_chunk, b_sems, e_sems, meta_sem, io_sem,
 ):
     z = lax.axis_index("inst")
     c = lax.axis_index("seq")
@@ -68,12 +69,17 @@
     def offset(d):
         return (z + d // 16) % 4, (y + (d // 4) % 4) % 4, (x + d % 4) % 4
 
+    def beside(e, py):
+        return (z + e // 4) % 4, py, (x + e % 4) % 4
+
     barrier = pltpu.get_barrier_semaphore()
 
-    @pl.loop(1, CHIPS)
-    def _(d):
-        pl.semaphore_signal(barrier, inc=1, device_id=place(*offset(d)), device_id_type=MESH)
-
+    @pl.loop(1, 16)
+    def _(e):
+        pl.semaphore_signal(barrier, inc=1, device_id=place(*beside(e, y)), device_id_type=MESH)
+
+    for m in range(1, 4):
+        pl.semaphore_signal(barrier, inc=1, device_id=place(z, (y + m) % 4, x), device_id_type=MESH)
     pl.semaphore_signal(barrier, inc=1, device_id=sibling, device_id_type=MESH)
 
     def key_copy(part):
@@ -99,27 +105,34 @@
     ).astype(BF16)
     nx[0] = jnp.concatenate([nk[0].astype(F32), nk[1].astype(F32)], axis=1)
 
-    pl.semaphore_wait(barrier, CHIPS)
+    pl.semaphore_wait(barrier, 19)
+
+    def shift(k):
+        return jnp.where(k == 1, 2, jnp.where(k == 2, 1, k))
 
     def turn(k):
-        return (y + k) % 4
-
-    def beside(e, py):
-        return (z + e // 4) % 4, py, (x + e % 4) % 4
-
-    def query_copy(k, e):
-        block = gat.at[core, y, spot]
+        return (y + shift(k)) % 4
+
+    def push(block, k, to):
         return pltpu.make_async_remote_copy(
             src_ref=block, dst_ref=block, send_sem=sg.at[k], recv_sem=rg.at[k],
-            device_id=place(*beside(e, (y + 4 - k) % 4)), device_id_type=MESH,
-        )
-
-    def plane_wait(k, blocks=16):
-        block = gat.at[core, turn(k), pl.ds(0, blocks)]
-        return pltpu.make_async_remote_copy(
-            src_ref=block, dst_ref=block, send_sem=sg.at[k], recv_sem=rg.at[k],
-            device_id=sibling, device_id_type=MESH,
-        )
+            device_id=to, device_id_type=MESH,
+        )
+
+    def plane_copy(e):
+        return push(gat.at[core, y, spot], 0, place(*beside(e, y)))
+
+    def across_copy():
+        return push(gat.at[core, y, spot], 4, place(z, (y + 2) % 4, x))
+
+    def relay_copy(e):
+        return push(gat.at[core, (y + 2) % 4, spot], 1, place(*beside(e, y)))
+
+    def next_copy(m):
+        return push(gat.at[core, y], 2 if m == 3 else 3, place(z, (y + m) % 4, x))
+
+    def arrived(k, plane, blocks):
+        return push(gat.at[core, plane, pl.ds(0, blocks)], k, sibling)
 
     def sib_copy(k, of):
         block = gat.at[of, turn(k)]
@@ -128,9 +141,11 @@
             device_id=sibling, device_id_type=MESH,
         )
 
-    @pl.loop(1, CHIPS)
-    def _(d):
-        query_copy(d // 16, d % 16).start()
+    across_copy().start()
+
+    @pl.loop(1, 16)
+    def _(e):
+        plane_copy(e).start()
 
     pair_rows = pltpu.make_async_remote_copy(
         src_ref=nx.at[0], dst_ref=nx.at[1], send_sem=n_sems.at[0], recv_sem=n_sems.at[1],
@@ -205,14 +220,23 @@
     def _():
         gnt[x % 2, shelf] = tile[...]
 
+    push(gat.at[core, (y + 2) % 4, spot], 4, sibling).wait_recv()
+
+    @pl.loop(1, 16)
+    def _(e):
+        relay_copy(e).start()
+
+    arrived(0, y, 15).wait_recv()
+    sib_copy(0, core).start()
+    for m in (3, 1):
+        next_copy(m).start()
+
     @pl.loop(0, 32)
     def _(half):
         @pl.when(2 * half + core > 0)
         def _():
             fresh_copy(2 * half + core).start()
 
-    plane_wait(0, 15).wait_recv()
-    sib_copy(0, core).start()
     meta_copy.wait()
 
     @pl.loop(0, KV_PARTS)
@@ -234,16 +258,23 @@
             device_id=sibling, device_id_type=MESH,
         )
 
-    def block_copy(to_chip, to):
-        return pltpu.make_async_remote_copy(
-            src_ref=sb.at[to_chip], dst_ref=rb.at[chip], send_sem=all_sems.at[0], recv_sem=all_sems.at[1],
+    def block_copy(k, at, to):
+        return pltpu.make_async_remote_copy(
+            src_ref=sb.at[turn(k), at], dst_ref=rb.at[y, spot], send_sem=b_sems.at[0, k], recv_sem=b_sems.at[1, k],
             device_id=to, device_id_type=MESH,
         )
 
-    def side_copy(to_chip, to):
-        return pltpu.make_async_remote_copy(
-            src_ref=ss.at[to_chip], dst_ref=rs.at[chip], send_sem=all_sems.at[2], recv_sem=all_sems.at[3],
+    def side_copy(k, at, to):
+        return pltpu.make_async_remote_copy(
+            src_ref=ss.at[turn(k), at], dst_ref=rs.at[y, spot], send_sem=e_sems.at[0, k], recv_sem=e_sems.at[1, k],
             device_id=to, device_id_type=MESH,
+        )
+
+    def all_copy(buf, sems, k):
+        block = buf.at[(y + 4 - SHIFT[k]) % 4, pl.ds(0, 16 if k else 15)]
+        return pltpu.make_async_remote_copy(
+            src_ref=block, dst_ref=block, send_sem=sems.at[0, k], recv_sem=sems.at[1, k],
+            device_id=sibling, device_id_type=MESH,
         )
 
     def scores(k):
@@ -334,7 +365,7 @@
                     packed[i] = jnp.where((lane4 >= to) & (lane4 < to + 8), there, packed[i])
         for i in range(4):
             for j in range(4):
-                ss[i * 16 + kt * 4 + j] = packed[i][j : j + 1, :]
+                ss[kt, i * 4 + j] = packed[i][j : j + 1, :]
         mt[...] = pltpu.roll(mt[...].T, (128 - core * 8) % 128, 1)
         chunk_copy(k).wait_recv()
 
@@ -350,7 +381,7 @@
                         s32[k, core, i, at, :] * factors[:, lane : lane + 1]
                         + r32[k, i, at, :] * factors[:, 32 + lane : 33 + lane]
                     )
-                sb[i * 16 + kt * 4 + j] = jnp.concatenate(total, axis=0).astype(BF16)
+                sb[kt, i * 4 + j] = jnp.concatenate(total, axis=0).astype(BF16)
 
     def send(k):
         kt = turn(k)
@@ -358,12 +389,23 @@
         @pl.loop(0, 16)
         def _(e):
             pz, _, px = beside(e, kt)
-            to_chip, to = pz * 16 + kt * 4 + px, place(pz, kt, px)
+            at, to = pz * 4 + px, place(pz, kt, px)
 
             @pl.when(k * 16 + e > 0)
             def _():
-                block_copy(to_chip, to).start()
-                side_copy(to_chip, to).start()
+                block_copy(k, at, to).start()
+                side_copy(k, at, to).start()
+
+    def pass_fresh():
+        @pl.when(core == 0)
+        def _():
+            fresh_wait(31).wait_recv()
+
+        @pl.when(core == 1)
+        def _():
+            fresh_wait(32).wait_recv()
+
+        sib_fresh(core).start()
 
     @pl.loop(0, 5)
     def _(k):
@@ -379,10 +421,11 @@
 
             most = scores(k)
 
-            @pl.when(k < 3)
-            def _():
-                plane_wait(k + 1).wait_recv()
-                sib_copy(k + 1, core).start()
+            for after, off, blocks in ((0, 2, 15), (1, 1, 16), (2, 3, 16)):
+                @pl.when(k == after)
+                def _():
+                    arrived(after + 1, (y + off) % 4, blocks).wait_recv()
+                    sib_copy(after + 1, core).start()
 
             @pl.when(k == 0)
             def _():
@@ -391,28 +434,20 @@
                     value_copy(part).wait()
 
             values(k, most)
+            hand_on(k)
 
         @pl.when(k > 0)
         def _():
             merge(k - 1)
             send(k - 1)
 
-        @pl.when(k < 4)
+        @pl.when(k == 3)
         def _():
-            hand_on(k)
-
-    rb[chip] = sb[chip]
-    rs[chip] = ss[chip]
-
-    @pl.when(core == 0)
-    def _():
-        fresh_wait(31).wait_recv()
-
-    @pl.when(core == 1)
-    def _():
-        fresh_wait(32).wait_recv()
-
-    sib_fresh(core).start()
+            pass_fresh()
+
+    rb[y, spot] = sb[y, spot]
+    rs[y, spot] = ss[y, spot]
+
     sib_fresh(sib).wait_recv()
 
     @pl.loop(0, 4)
@@ -457,35 +492,27 @@
     new_den = jnp.concatenate(new_den, axis=0)
     new_num = jnp.concatenate(new_num, axis=0)
 
-    most = pl.ds(0, CHIPS - 1)
-    all_blocks = pltpu.make_async_remote_copy(
-        src_ref=sb.at[most], dst_ref=rb.at[most], send_sem=all_sems.at[0], recv_sem=all_sems.at[1],
-        device_id=sibling, device_id_type=MESH,
-    )
-    all_sides = pltpu.make_async_remote_copy(
-        src_ref=ss.at[most], dst_ref=rs.at[most], send_sem=all_sems.at[2], recv_sem=all_sems.at[3],
-        device_id=sibling, device_id_type=MESH,
-    )
-    all_sides.wait_recv()
-    side = rs[...].reshape(CHIPS, 128)
-    side = jnp.concatenate([side, jnp.zeros((128 - CHIPS, 128), F32)], axis=0).T
-    side_m, side_den = side[0:32, :CHIPS], side[32:64, :CHIPS]
-    final_m = jnp.maximum(jnp.max(side_m, axis=1, keepdims=True), new_m)
-    scales = jnp.exp(side_m - final_m)
-    new_scale = jnp.exp(new_m - final_m)
-    final_den = jnp.sum(scales * side_den, axis=1, keepdims=True) + new_den * new_scale
-    total = new_num * new_scale
-    all_blocks.wait_recv()
-    scales = jnp.concatenate([scales, jnp.zeros((32, 128 - CHIPS), F32)], axis=1)
-
-    @pl.loop(0, CHIPS // 8, init_carry=(total, scales))
-    def total_and_scales(group, carry):
-        total, scales = carry
-        for e in range(8):
-            total = total + scales[:, e : e + 1] * rb[group * 8 + e].astype(F32)
-        return total, pltpu.roll(scales, 120, 1)
-
-    total = total_and_scales[0]
+    def take_in(phases, top, den, total):
+        planes = [(y + 4 - SHIFT[k]) % 4 for k in phases]
+        count = 16 * len(phases)
+        for k in phases:
+            all_copy(rs, e_sems, k).wait_recv()
+        side = [rs[plane].reshape(16, 128) for plane in planes]
+        side = jnp.concatenate(side + [jnp.zeros((128 - count, 128), F32)], axis=0).T
+        side_m, side_den = side[0:32, :count], side[32:64, :count]
+        new_top = jnp.maximum(jnp.max(side_m, axis=1, keepdims=True), top)
+        scales = jnp.exp(side_m - new_top)
+        old_scale = jnp.exp(top - new_top)
+        den = jnp.sum(scales * side_den, axis=1, keepdims=True) + den * old_scale
+        total = total * old_scale
+        for k, plane in enumerate(planes):
+            all_copy(rb, b_sems, phases[k]).wait_recv()
+            for e in range(16):
+                total = total + scales[:, k * 16 + e : k * 16 + e + 1] * rb[plane, e].astype(F32)
+        return new_top, den, total
+
+    state = take_in((0, 1, 2), new_m, new_den, new_num)
+    _, final_den, total = take_in((3,), *state)
     result = total / final_den
     for t in range(4):
         out[t // 2, :, (t % 2) * 128 : (t % 2) * 128 + 128] = result[t * 8 : t * 8 + 8].astype(BF16)
@@ -497,11 +524,14 @@
     for store in stores:
         store.start()
 
-    all_blocks.wait_send()
-    all_sides.wait_send()
-    plane_wait(0, 15).wait_send()
-    for k in range(1, 4):
-        plane_wait(k).wait_send()
+    for k in range(4):
+        all_copy(sb, b_sems, k).wait_send()
+        all_copy(ss, e_sems, k).wait_send()
+    across_copy().wait_send()
+    arrived(0, y, 15).wait_send()
+    arrived(1, y, 15).wait_send()
+    for m in (3, 1):
+        next_copy(m).wait_send()
     for k in range(4):
         sib_copy(k, core).wait_send()
         peak_copy(k).wait_send()
@@ -570,18 +600,18 @@
             pltpu.VMEM((32, 128), F32),
             pltpu.VMEM((4, 2, 4, 128, 128), F32),
             pltpu.VMEM((4, 4, 128, 128), F32),
-            pltpu.VMEM((CHIPS, 32, 128), BF16),
-            pltpu.VMEM((CHIPS, 32, 128), BF16),
-            pltpu.VMEM((CHIPS, 1, 128), F32),
-            pltpu.VMEM((CHIPS, 1, 128), F32),
+            pltpu.VMEM((4, 16, 32, 128), BF16),
+            pltpu.VMEM((4, 16, 32, 128), BF16),
+            pltpu.VMEM((4, 16, 1, 128), F32),
+            pltpu.VMEM((4, 16, 1, 128), F32),
             pltpu.VMEM((64, 128), F32),
             pltpu.VMEM((40, 128), I32),
             pltpu.SMEM((40, 128), I32),
             pltpu.VMEM((40, 128), I32),
             dma((KV_PARTS,)),
             dma((KV_PARTS,)),
-            dma((4,)),
-            dma((4,)),
+            dma((5,)),
+            dma((5,)),
             dma((4,)),
             dma((4,)),
             dma((6,)),
@@ -589,7 +619,8 @@
             dma((4,)),
             dma((4,)),
             dma((4,)),
-            dma((4,)),
+            dma((2, 4)),
+            dma((2, 4)),
             dma,
             dma((7,)),
         ],

time: 43.8 us -> 38.5 us (0.88)
  Pallas kernels: 43.1 us -> 37.7 us
    pallas_call x1, Pallas kernels: 41.2 us -> 35.8 us  [per_device(): pl.pallas_call(kernel, out_shape=(jax.ShapeDtypeStruct((2, 8, 256), BF16)...]
where the time goes in v5:
time: 38.5 us; the launch traced here: 38.4 us
  Pallas kernels  37.7 us (98%)
  between operations  0.64 us (2%)
    pallas_call x1, Pallas kernels, per_device(): pl.pallas_call(kernel, out_shape=(jax.ShapeDtypeStruct((2, 8, 256), BF16)...  35.8 us
    pallas_call x1, Pallas kernels, per_device(): pl.pallas_call(hand_over, out_shape=(jax.ShapeDtypeStruct((2, 8, 256), BF...  1.87 us

profile of v5, /device:TPU:1, one launch (start us, length us, event | category | flops | bytes accessed | tf_op | source)
XLA Modules:
  0.0 38.4 jit_solution(17816701252523569834)
XLA Ops:
  0.6 35.8 %shard_map.95 = (bf16[2,8,256]{2,1,0:T(8,128)(2,1)}, bf16[4,2048]{1,0:T(4,128)(2,1)}) custom-call(bf16[32,128,2048]{2,1,0:T(8,128)(2,1)} %kv.1, bf16[2,8,256]{2,1,0:T(8,128)(2,1)} %q_in.1, bf16[2,8,64]{2,1,0:T(8,128)(2,1)} %nk_in.1, s32[32,128]{1,0:T(8,128)} %dev_in.1, s32[32,128]{1,0:T(8,128)} %slot_in.1, s32[2,32]{1,0:T(2,128)} %own_dev_in.1, ...), custom_call_target="tpu_custom_call" | custom-call | tf_op jit(solution)/shard_map/pallas_call | solution.py:568
  36.5 1.9 %shard_map.96 = (bf16[2,8,256]{2,1,0:T(8,128)(2,1)}, bf16[4,2048]{1,0:T(4,128)(2,1)}) custom-call(bf16[2,8,256]{2,1,0:T(8,128)(2,1)} %get-tuple-element.4.result, bf16[4,2048]{1,0:T(4,128)(2,1)} %get-tuple-element.5.rows), custom_call_target="tpu_custom_call" | custom-call | tf_op jit(solution)/shard_map/pallas_call | solution.py:631

commit v6 on v5

--- a/solution.py
+++ b/solution.py
@@ -42,12 +42,13 @@
 def kernel(
     kv, q_in, nk_in, dev_in, slot_in, own_dev_in, own_row_in, lens_in, out_at, tail_at,
     q, nk, dev, slot, own_dev, own_row, lens, out, tail,
-    kvb, gat, nx, tile, gnt, gq, gn, wb, pk, dn, cb, mx, mxr, mt, uw, s32, r32, sb, rb, ss, rs, tl, meta, smeta, codes,
+    info, kvb, gat, nx, tile, gnt, gq, gn, wb, pk, dn, cb, mx, mxr, mt, lift, uw, s32, r32, sb, rb, ss, rs, tl, meta, smeta, codes,
     k_sem, v_sem, sg, rg, s_sib, r_sib, n_sems, s_m, r_m, s_chunk, r_chunk, b_sems, e_sems, meta_sem, io_sem,
 ):
     z = lax.axis_index("inst")
     c = lax.axis_index("seq")
-    y, x, core = c // 8, (c // 2) % 4, c % 2
+    y, x, core = c >> 3, (c >> 1) & 3, c & 1
+    zs, ys, xs = [[(v + d) & 3 for d in range(4)] for v in (z, y, x)]
     me = z * 32 + c
     chip = z * 16 + y * 4 + x
     sib = 1 - core
@@ -63,24 +64,21 @@
             (own_dev_in, own_dev), (own_row_in, own_row), (lens_in, lens),
         ])
     ]
-    for load in loads:
+    for load in loads[:2]:
         load.start()
 
-    def offset(d):
-        return (z + d // 16) % 4, (y + (d // 4) % 4) % 4, (x + d % 4) % 4
-
     def beside(e, py):
-        return (z + e // 4) % 4, py, (x + e % 4) % 4
+        return zs[e // 4], py, xs[e % 4]
 
     barrier = pltpu.get_barrier_semaphore()
 
-    @pl.loop(1, 16)
-    def _(e):
+    for e in range(1, 16):
         pl.semaphore_signal(barrier, inc=1, device_id=place(*beside(e, y)), device_id_type=MESH)
-
     for m in range(1, 4):
-        pl.semaphore_signal(barrier, inc=1, device_id=place(z, (y + m) % 4, x), device_id_type=MESH)
+        pl.semaphore_signal(barrier, inc=1, device_id=place(z, ys[m], x), device_id_type=MESH)
     pl.semaphore_signal(barrier, inc=1, device_id=sibling, device_id_type=MESH)
+    for load in loads[2:]:
+        load.start()
 
     def key_copy(part):
         span = pl.ds(part * UNROLL, UNROLL)
@@ -107,11 +105,8 @@
 
     pl.semaphore_wait(barrier, 19)
 
-    def shift(k):
-        return jnp.where(k == 1, 2, jnp.where(k == 2, 1, k))
-
     def turn(k):
-        return (y + shift(k)) % 4
+        return (y + ((k & 1) << 1) + (k >> 1)) & 3
 
     def push(block, k, to):
         return pltpu.make_async_remote_copy(
@@ -123,13 +118,13 @@
         return push(gat.at[core, y, spot], 0, place(*beside(e, y)))
 
     def across_copy():
-        return push(gat.at[core, y, spot], 4, place(z, (y + 2) % 4, x))
+        return push(gat.at[core, y, spot], 4, place(z, ys[2], x))
 
     def relay_copy(e):
-        return push(gat.at[core, (y + 2) % 4, spot], 1, place(*beside(e, y)))
+        return push(gat.at[core, ys[2], spot], 1, place(*beside(e, y)))
 
     def next_copy(m):
-        return push(gat.at[core, y], 2 if m == 3 else 3, place(z, (y + m) % 4, x))
+        return push(gat.at[core, y], 2 if m == 3 else 3, place(z, ys[m], x))
 
     def arrived(k, plane, blocks):
         return push(gat.at[core, plane, pl.ds(0, blocks)], k, sibling)
@@ -143,8 +138,7 @@
 
     across_copy().start()
 
-    @pl.loop(1, 16)
-    def _(e):
+    for e in range(1, 16):
         plane_copy(e).start()
 
     pair_rows = pltpu.make_async_remote_copy(
@@ -152,25 +146,40 @@
         device_id=sibling, device_id_type=MESH,
     )
     pair_rows.start()
-    shelf = z * 8 + y * 2 + x // 2
-
-    def fresh_copy(d):
-        return pltpu.make_async_remote_copy(
-            src_ref=tile, dst_ref=gnt.at[x % 2, shelf], send_sem=n_sems.at[2], recv_sem=n_sems.at[3],
-            device_id=place(*offset(d)), device_id_type=MESH,
-        )
-
-    def fresh_wait(blocks):
-        block = gnt.at[0, pl.ds(0, blocks)]
+    shelf = z * 2 + (x >> 1)
+    side_of = (x + core) & 1
+
+    def fresh_copy(e):
+        return pltpu.make_async_remote_copy(
+            src_ref=tile, dst_ref=gnt.at[y, x & 1, shelf], send_sem=n_sems.at[2], recv_sem=n_sems.at[3],
+            device_id=place(*beside(e, y)), device_id_type=MESH,
+        )
+
+    def fresh_wait(tiles):
+        block = gnt.at[y, side_of, pl.ds(0, tiles)]
         return pltpu.make_async_remote_copy(
             src_ref=block, dst_ref=block, send_sem=n_sems.at[2], recv_sem=n_sems.at[3],
             device_id=sibling, device_id_type=MESH,
         )
 
+    def fresh_plane(m):
+        block = gnt.at[y, side_of]
+        return pltpu.make_async_remote_copy(
+            src_ref=block, dst_ref=block, send_sem=n_sems.at[4], recv_sem=n_sems.at[5],
+            device_id=place(z, ys[m], x), device_id_type=MESH,
+        )
+
+    def fresh_planes():
+        block = gnt.at[pl.ds(0, 3), side_of]
+        return pltpu.make_async_remote_copy(
+            src_ref=block, dst_ref=block, send_sem=n_sems.at[4], recv_sem=n_sems.at[5],
+            device_id=sibling, device_id_type=MESH,
+        )
+
     def sib_fresh(of):
-        block = gnt.at[(x + of) % 2]
-        return pltpu.make_async_remote_copy(
-            src_ref=block, dst_ref=block, send_sem=n_sems.at[4], recv_sem=n_sems.at[5],
+        block = gnt.at[:, (x + of) & 1]
+        return pltpu.make_async_remote_copy(
+            src_ref=block, dst_ref=block, send_sem=n_sems.at[6], recv_sem=n_sems.at[7],
             device_id=sibling, device_id_type=MESH,
         )
 
@@ -218,12 +227,11 @@
 
     @pl.when(core == 0)
     def _():
-        gnt[x % 2, shelf] = tile[...]
-
-    push(gat.at[core, (y + 2) % 4, spot], 4, sibling).wait_recv()
-
-    @pl.loop(1, 16)
-    def _(e):
+        gnt[y, x & 1, shelf] = tile[...]
+
+    push(gat.at[core, ys[2], spot], 4, sibling).wait_recv()
+
+    for e in range(1, 16):
         relay_copy(e).start()
 
     arrived(0, y, 15).wait_recv()
@@ -231,13 +239,28 @@
     for m in (3, 1):
         next_copy(m).start()
 
-    @pl.loop(0, 32)
-    def _(half):
-        @pl.when(2 * half + core > 0)
-        def _():
-            fresh_copy(2 * half + core).start()
+    for of in range(2):
+        @pl.when(core == of)
+        def _():
+            for e in range(2 - of, 16, 2):
+                fresh_copy(e).start()
 
     meta_copy.wait()
+
+    @pl.loop(0, SLOTS)
+    def _(n):
+        req, held, prev, end = smeta[n, 0], smeta[n, 1], smeta[n, 2], smeta[n, 3]
+        r = jnp.maximum(req, 0)
+        b = (jnp.maximum(held, 1) - 1) & 127
+        info[0, n] = req
+        info[1, n] = r >> 3
+        info[2, n] = r & 7
+        info[3, n] = jnp.where(held > 0, lens[r] - b * 128, 0)
+        info[4, n] = prev
+        info[5, n] = jnp.maximum(prev, 0)
+        info[6, n] = end
+        info[7, n] = jnp.maximum(end, 0)
+
 
     @pl.loop(0, KV_PARTS)
     def _(part):
@@ -271,7 +294,7 @@
         )
 
     def all_copy(buf, sems, k):
-        block = buf.at[(y + 4 - SHIFT[k]) % 4, pl.ds(0, 16 if k else 15)]
+        block = buf.at[ys[(4 - SHIFT[k]) % 4], pl.ds(0, 16 if k else 15)]
         return pltpu.make_async_remote_copy(
             src_ref=block, dst_ref=block, send_sem=sems.at[0, k], recv_sem=sems.at[1, k],
             device_id=sibling, device_id_type=MESH,
@@ -284,10 +307,8 @@
         def most(group, most):
             for e in range(GROUP):
                 n = group * GROUP + e
-                r = jnp.maximum(smeta[n, 0], 0)
-                b = (jnp.maximum(smeta[n, 1], 1) - 1) % 128
-                count = jnp.where(smeta[n, 1] > 0, lens[r] - b * 128, 0)
-                parts = [gq[of, r // 8, pl.ds(r % 8, 16, stride=8), :].reshape(2, 8, 128) for of in range(2)]
+                i, rl, count = info[1, n], info[2, n], info[3, n]
+                parts = [gq[of, i, pl.ds(rl, 16, stride=8), :].reshape(2, 8, 128) for of in range(2)]
                 heads = jnp.concatenate(parts, axis=1).astype(BF16)
                 first = jnp.concatenate([heads[0], blank], axis=1)
                 second = jnp.concatenate([blank, heads[1]], axis=1)
@@ -295,32 +316,31 @@
                     jnp.concatenate([first, second], axis=0), kvb[n, :, cols],
                     (((1,), (1,)), ((), ())), preferred_element_type=F32,
                 )
-                valid = lanes < count
-                score = jnp.where(valid, score * SCALE, LOW)
+                score = jnp.where(lanes < count, score * SCALE, LOW)
                 peak = jnp.max(score, axis=1, keepdims=True)
-                w = jnp.where(valid, jnp.exp(score - peak), 0.0).astype(BF16)
-                wb[n] = w
+                wb[n] = jnp.exp(score - peak).astype(BF16)
                 pk[n] = jnp.broadcast_to(peak, (32, 128))
-                dn[n] = jnp.broadcast_to(jnp.sum(w.astype(F32), axis=1, keepdims=True), (32, 128))
-                most = jnp.where(lanes == smeta[n, 0], jnp.maximum(most, peak), most)
+                most = jnp.where(lanes == info[0, n], jnp.maximum(most, peak), most)
             return most
 
         return most
 
     def values(k, most):
         cols = pl.ds(pl.multiple_of(1024 + turn(k) * 256, 256), 256)
+        dn[...] = jnp.dot(
+            wb[...].reshape(SLOTS * 32, 128), jnp.ones((128, 128), BF16), preferred_element_type=F32
+        ).reshape(SLOTS, 32, 128)
 
         @pl.loop(0, SLOTS // GROUP, init_carry=jnp.zeros((32, 128), F32))
         def den(group, den):
             for e in range(GROUP):
                 n = group * GROUP + e
-                r = smeta[n, 0]
+                r = info[0, n]
                 best = jnp.max(jnp.where(lanes == r, most, LOW), axis=1, keepdims=True)
                 factor = jnp.exp(pk[n] - best)
                 both = jnp.dot(wb[n], kvb[n, :, cols], preferred_element_type=F32)
                 num = jnp.concatenate([both[:16, :128], both[16:, 128:]], axis=0)
-                prev = smeta[n, 2]
-                earlier = jnp.where(prev >= 0, cb[jnp.maximum(prev, 0)], 0.0)
+                earlier = jnp.where(info[4, n] >= 0, cb[info[5, n]], 0.0)
                 cb[n] = num * factor + earlier
                 den = den + jnp.where(lanes == r, factor * dn[n], 0.0)
             return den
@@ -333,8 +353,7 @@
         @pl.loop(0, 4)
         def _(i):
             for rl in range(8):
-                end = smeta[i * 8 + rl, 3]
-                sums = jnp.where(end >= 0, cb[jnp.maximum(end, 0)], 0.0)
+                sums = jnp.where(info[6, i * 8 + rl] >= 0, cb[info[7, i * 8 + rl]], 0.0)
                 for xh in range(2):
                     for of in range(2):
                         at = pl.ds(xh * 64 + rl, 8, stride=8)
@@ -349,10 +368,11 @@
         chip_top = jnp.maximum(top, other)
         mine_f, other_f = jnp.exp(top - chip_top), jnp.exp(other - chip_top)
         chip_den = mx[k, 1] * mine_f + mxr[k, 1] * other_f
-        mt[...] = jnp.concatenate([mine_f, other_f, chip_top, chip_den], axis=0)
+        mt[0:32, :] = chip_top
+        mt[32:64, :] = chip_den
         for w in range(2):
             for xh in range(2):
-                row = pl.multiple_of(64 + w * 32 + xh * 16 + core * 8, 8)
+                row = pl.multiple_of(w * 32 + xh * 16 + core * 8, 8)
                 uw[w * 16 + xh * 8 : w * 16 + xh * 8 + 8, :] = mt[pl.ds(row, 8), :]
         lane4 = iota((4, 128), 1)
         packed = [jnp.zeros((4, 128), F32) for _ in range(4)]
@@ -366,12 +386,13 @@
         for i in range(4):
             for j in range(4):
                 ss[kt, i * 4 + j] = packed[i][j : j + 1, :]
-        mt[...] = pltpu.roll(mt[...].T, (128 - core * 8) % 128, 1)
+        both_f = jnp.concatenate([mine_f, other_f, jnp.zeros((64, 128), F32)], axis=0).T
+        lift[...] = pltpu.roll(both_f[0:32], (128 - core * 8) % 128, 1)
         chunk_copy(k).wait_recv()
 
         @pl.loop(0, 4)
         def _(i):
-            factors = mt[pl.ds(pl.multiple_of(i * 8, 8), 8), :]
+            factors = lift[pl.ds(pl.multiple_of(i * 8, 8), 8), :]
             for j in range(4):
                 total = []
                 for t in range(4):
@@ -386,25 +407,33 @@
     def send(k):
         kt = turn(k)
 
-        @pl.loop(0, 16)
-        def _(e):
+        def one(e):
             pz, _, px = beside(e, kt)
             at, to = pz * 4 + px, place(pz, kt, px)
-
-            @pl.when(k * 16 + e > 0)
-            def _():
-                block_copy(k, at, to).start()
-                side_copy(k, at, to).start()
+            block_copy(k, at, to).start()
+            side_copy(k, at, to).start()
+
+        @pl.when(k > 0)
+        def _():
+            one(0)
+
+        for e in range(1, 16):
+            one(e)
+
+    def spread_fresh():
+        @pl.when(core == 0)
+        def _():
+            fresh_wait(7).wait_recv()
+
+        @pl.when(core == 1)
+        def _():
+            fresh_wait(8).wait_recv()
+
+        for m in range(1, 4):
+            fresh_plane(m).start()
 
     def pass_fresh():
-        @pl.when(core == 0)
-        def _():
-            fresh_wait(31).wait_recv()
-
-        @pl.when(core == 1)
-        def _():
-            fresh_wait(32).wait_recv()
-
+        fresh_planes().wait_recv()
         sib_fresh(core).start()
 
     @pl.loop(0, 5)
@@ -415,7 +444,7 @@
 
             @pl.loop(0, 8)
             def _(part):
-                of, i = part // 4, part % 4
+                of, i = part >> 2, part & 3
                 for j in range(4):
                     gq[of, i, j * 32 : j * 32 + 32, :] = gat[of, turn(k), i * 4 + j].astype(F32)
 
@@ -424,7 +453,7 @@
             for after, off, blocks in ((0, 2, 15), (1, 1, 16), (2, 3, 16)):
                 @pl.when(k == after)
                 def _():
-                    arrived(after + 1, (y + off) % 4, blocks).wait_recv()
+                    arrived(after + 1, ys[off], blocks).wait_recv()
                     sib_copy(after + 1, core).start()
 
             @pl.when(k == 0)
@@ -441,6 +470,10 @@
             merge(k - 1)
             send(k - 1)
 
+        @pl.when(k == 1)
+        def _():
+            spread_fresh()
+
         @pl.when(k == 3)
         def _():
             pass_fresh()
@@ -453,7 +486,7 @@
     @pl.loop(0, 4)
     def _(i):
         for j in range(16):
-            fresh = gnt[j % 2, i * 8 + j // 2].astype(F32)
+            fresh = gnt[j // 4, j % 2, i * 2 + (j % 4) // 2].astype(F32)
             for of in range(2):
                 gn[of, i, j * 8 : j * 8 + 8, :] = fresh[of * 8 : of * 8 + 8]
 
@@ -461,8 +494,8 @@
     def _(e):
         found_row = smeta[SLOTS + e, 0]
         which = jnp.maximum(found_row - 1, 0)
-        late, r = which // 32, which % 32
-        pair = [gn[of, r // 8, pl.ds(r % 8, 16, stride=8), :] for of in range(2)]
+        late, r = which >> 5, which & 31
+        pair = [gn[of, r >> 3, pl.ds(r & 7, 16, stride=8), :] for of in range(2)]
         tl[pl.ds(pl.multiple_of(e * 16, 16), 16), :] = jnp.where(found_row > 0, halves(pair[0], pair[1], late > 0), 0.0)
     for j in range(16):
         tail[:, j * 128 : j * 128 + 128] = tl[pl.ds(j, 4, stride=16), :].astype(BF16)
@@ -493,7 +526,7 @@
     new_num = jnp.concatenate(new_num, axis=0)
 
     def take_in(phases, top, den, total):
-        planes = [(y + 4 - SHIFT[k]) % 4 for k in phases]
+        planes = [ys[(4 - SHIFT[k]) % 4] for k in phases]
         count = 16 * len(phases)
         for k in phases:
             all_copy(rs, e_sems, k).wait_recv()
@@ -540,12 +573,13 @@
 
     @pl.when(core == 0)
     def _():
-        fresh_wait(31).wait_send()
+        fresh_wait(7).wait_send()
 
     @pl.when(core == 1)
     def _():
-        fresh_wait(32).wait_send()
-
+        fresh_wait(8).wait_send()
+
+    fresh_planes().wait_send()
     sib_fresh(core).wait_send()
     for store in stores:
         store.wait()
@@ -583,11 +617,12 @@
             pltpu.SMEM((REQS,), I32),
             pltpu.VMEM((2, 8, 256), BF16),
             pltpu.VMEM((4, 2048), BF16),
+            pltpu.SMEM((8, SLOTS), I32),
             pltpu.VMEM((SLOTS, 128, 2048), BF16),
             pltpu.VMEM((2, 4, 16, 32, 128), BF16),
             pltpu.VMEM((2, 8, 128), F32),
             pltpu.VMEM((16, 128), BF16),
-            pltpu.VMEM((2, 32, 16, 128), BF16),
+            pltpu.VMEM((4, 2, 8, 16, 128), BF16),
             pltpu.VMEM((2, 4, 128, 128), F32),
             pltpu.VMEM((2, 4, 128, 128), F32),
             pltpu.VMEM((SLOTS, 32, 128), BF16),
@@ -596,7 +631,8 @@
             pltpu.VMEM((SLOTS, 32, 128), F32),
             pltpu.VMEM((4, 2, 32, 128), F32),
             pltpu.VMEM((4, 2, 32, 128), F32),
-            pltpu.VMEM((128, 128), F32),
+            pltpu.VMEM((64, 128), F32),
+            pltpu.VMEM((32, 128), F32),
             pltpu.VMEM((32, 128), F32),
             pltpu.VMEM((4, 2, 4, 128, 128), F32),
             pltpu.VMEM((4, 4, 128, 128), F32),
@@ -614,7 +650,7 @@
             dma((5,)),
             dma((4,)),
             dma((4,)),
-            dma((6,)),
+            dma((8,)),
             dma((4,)),
             dma((4,)),
             dma((4,)),

time: 38.5 us -> 37.1 us (0.964)
  Pallas kernels: 37.7 us -> 36.3 us
    pallas_call x1, Pallas kernels: 35.8 us -> 34.5 us  [per_device(): pl.pallas_call(kernel, out_shape=(jax.ShapeDtypeStruct((2, 8, 256), BF16)...]
where the time goes in v6:
time: 37.1 us; the launch traced here: 37 us
  Pallas kernels  36.3 us (98%)
  between operations  0.64 us (2%)
    pallas_call x1, Pallas kernels, per_device(): pl.pallas_call(kernel, out_shape=(jax.ShapeDtypeStruct((2, 8, 256), BF16)...  34.5 us
    pallas_call x1, Pallas kernels, per_device(): pl.pallas_call(hand_over, out_shape=(jax.ShapeDtypeStruct((2, 8, 256), BF...  1.87 us

profile of v6, /device:TPU:1, one launch (start us, length us, event | category | flops | bytes accessed | tf_op | source)
XLA Modules:
  0.0 37.0 jit_solution(15876735567718358715)
XLA Ops:
  0.6 34.5 %shard_map.95 = (bf16[2,8,256]{2,1,0:T(8,128)(2,1)}, bf16[4,2048]{1,0:T(4,128)(2,1)}) custom-call(bf16[32,128,2048]{2,1,0:T(8,128)(2,1)} %kv.1, bf16[2,8,256]{2,1,0:T(8,128)(2,1)} %q_in.1, bf16[2,8,64]{2,1,0:T(8,128)(2,1)} %nk_in.1, s32[32,128]{1,0:T(8,128)} %dev_in.1, s32[32,128]{1,0:T(8,128)} %slot_in.1, s32[2,32]{1,0:T(2,128)} %own_dev_in.1, ...), custom_call_target="tpu_custom_call" | custom-call | tf_op jit(solution)/shard_map/pallas_call | solution.py:602
  35.1 1.9 %shard_map.96 = (bf16[2,8,256]{2,1,0:T(8,128)(2,1)}, bf16[4,2048]{1,0:T(4,128)(2,1)}) custom-call(bf16[2,8,256]{2,1,0:T(8,128)(2,1)} %get-tuple-element.4.result, bf16[4,2048]{1,0:T(4,128)(2,1)} %get-tuple-element.5.rows), custom_call_target="tpu_custom_call" | custom-call | tf_op jit(solution)/shard_map/pallas_call | solution.py:667

commit v7 on v6

--- a/solution.py
+++ b/solution.py
@@ -19,7 +19,7 @@
 LOW = -1e30
 SCALE = 1.0 / math.sqrt(128)
 UNROLL = 4
-GROUP = 32
+GROUP = 16
 SHIFT = (0, 2, 1, 3)
 KV_PARTS = SLOTS // UNROLL
 

time: 37.1 us -> 38.3 us (1.032)
  Pallas kernels: 36.3 us -> 37.5 us
    pallas_call x1, Pallas kernels: 34.5 us -> 35.7 us  [per_device(): pl.pallas_call(kernel, out_shape=(jax.ShapeDtypeStruct((2, 8, 256), BF16)...]
where the time goes in v7:
time: 38.3 us; the launch traced here: 38.2 us
  Pallas kernels  37.5 us (98%)
  between operations  0.64 us (2%)
    pallas_call x1, Pallas kernels, per_device(): pl.pallas_call(kernel, out_shape=(jax.ShapeDtypeStruct((2, 8, 256), BF16)...  35.7 us
    pallas_call x1, Pallas kernels, per_device(): pl.pallas_call(hand_over, out_shape=(jax.ShapeDtypeStruct((2, 8, 256), BF...  1.87 us

profile of v7, /device:TPU:1, one launch (start us, length us, event | category | flops | bytes accessed | tf_op | source)
XLA Modules:
  0.0 38.2 jit_solution(9994936353178225133)
XLA Ops:
  0.6 35.7 %shard_map.95 = (bf16[2,8,256]{2,1,0:T(8,128)(2,1)}, bf16[4,2048]{1,0:T(4,128)(2,1)}) custom-call(bf16[32,128,2048]{2,1,0:T(8,128)(2,1)} %kv.1, bf16[2,8,256]{2,1,0:T(8,128)(2,1)} %q_in.1, bf16[2,8,64]{2,1,0:T(8,128)(2,1)} %nk_in.1, s32[32,128]{1,0:T(8,128)} %dev_in.1, s32[32,128]{1,0:T(8,128)} %slot_in.1, s32[2,32]{1,0:T(2,128)} %own_dev_in.1, ...), custom_call_target="tpu_custom_call" | custom-call | tf_op jit(solution)/shard_map/pallas_call | solution.py:602
  36.3 1.9 %shard_map.96 = (bf16[2,8,256]{2,1,0:T(8,128)(2,1)}, bf16[4,2048]{1,0:T(4,128)(2,1)}) custom-call(bf16[2,8,256]{2,1,0:T(8,128)(2,1)} %get-tuple-element.4.result, bf16[4,2048]{1,0:T(4,128)(2,1)} %get-tuple-element.5.rows), custom_call_target="tpu_custom_call" | custom-call | tf_op jit(solution)/shard_map/pallas_call | solution.py:667

commit v8 on v6

--- a/solution.py
+++ b/solution.py
@@ -21,6 +21,7 @@
 UNROLL = 4
 GROUP = 32
 SHIFT = (0, 2, 1, 3)
+PLACES = (10, 9, 11, 6, 14, 2, 8, 5, 7, 13, 15, 1, 3, 4, 12)
 KV_PARTS = SLOTS // UNROLL
 
 
@@ -72,7 +73,7 @@
 
     barrier = pltpu.get_barrier_semaphore()
 
-    for e in range(1, 16):
+    for e in PLACES:
         pl.semaphore_signal(barrier, inc=1, device_id=place(*beside(e, y)), device_id_type=MESH)
     for m in range(1, 4):
         pl.semaphore_signal(barrier, inc=1, device_id=place(z, ys[m], x), device_id_type=MESH)
@@ -89,10 +90,6 @@
         span = pl.ds(part * UNROLL, UNROLL)
         cols = pl.ds(1024, 1024)
         return pltpu.make_async_copy(kv.at[span, :, cols], kvb.at[span, :, cols], v_sem.at[part])
-
-    @pl.loop(0, KV_PARTS)
-    def _(part):
-        key_copy(part).start()
 
     spot = z * 4 + x
     for load in loads[:2]:
@@ -138,8 +135,12 @@
 
     across_copy().start()
 
-    for e in range(1, 16):
+    for e in PLACES:
         plane_copy(e).start()
+
+    @pl.loop(0, KV_PARTS)
+    def _(part):
+        key_copy(part).start()
 
     pair_rows = pltpu.make_async_remote_copy(
         src_ref=nx.at[0], dst_ref=nx.at[1], send_sem=n_sems.at[0], recv_sem=n_sems.at[1],
@@ -231,7 +232,7 @@
 
     push(gat.at[core, ys[2], spot], 4, sibling).wait_recv()
 
-    for e in range(1, 16):
+    for e in PLACES:
         relay_copy(e).start()
 
     arrived(0, y, 15).wait_recv()
@@ -350,8 +351,7 @@
         peak_copy(k).start()
 
     def hand_on(k):
-        @pl.loop(0, 4)
-        def _(i):
+        for i in range(4):
             for rl in range(8):
                 sums = jnp.where(info[6, i * 8 + rl] >= 0, cb[info[7, i * 8 + rl]], 0.0)
                 for xh in range(2):
@@ -390,9 +390,8 @@
         lift[...] = pltpu.roll(both_f[0:32], (128 - core * 8) % 128, 1)
         chunk_copy(k).wait_recv()
 
-        @pl.loop(0, 4)
-        def _(i):
-            factors = lift[pl.ds(pl.multiple_of(i * 8, 8), 8), :]
+        for i in range(4):
+            factors = lift[i * 8 : i * 8 + 8, :]
             for j in range(4):
                 total = []
                 for t in range(4):
@@ -413,12 +412,12 @@
             block_copy(k, at, to).start()
             side_copy(k, at, to).start()
 
+        for e in PLACES:
+            one(e)
+
         @pl.when(k > 0)
         def _():
             one(0)
-
-        for e in range(1, 16):
-            one(e)
 
     def spread_fresh():
         @pl.when(core == 0)
@@ -442,19 +441,24 @@
         def _():
             sib_copy(k, sib).wait_recv()
 
-            @pl.loop(0, 8)
-            def _(part):
-                of, i = part >> 2, part & 3
-                for j in range(4):
-                    gq[of, i, j * 32 : j * 32 + 32, :] = gat[of, turn(k), i * 4 + j].astype(F32)
+            kt = turn(k)
+            for of in range(2):
+                for i in range(4):
+                    for j in range(4):
+                        gq[of, i, j * 32 : j * 32 + 32, :] = gat[of, kt, i * 4 + j].astype(F32)
 
             most = scores(k)
 
-            for after, off, blocks in ((0, 2, 15), (1, 1, 16), (2, 3, 16)):
-                @pl.when(k == after)
-                def _():
-                    arrived(after + 1, ys[off], blocks).wait_recv()
-                    sib_copy(after + 1, core).start()
+            @pl.when(k == 0)
+            def _():
+                arrived(1, ys[2], 15).wait_recv()
+                sib_copy(1, core).start()
+
+            @pl.when(k == 1)
+            def _():
+                for phase in (2, 3):
+                    arrived(phase, ys[SHIFT[phase]], 16).wait_recv()
+                    sib_copy(phase, core).start()
 
             @pl.when(k == 0)
             def _():

time: 37.1 us -> 35.6 us (0.960)
  Pallas kernels: 36.3 us -> 34.8 us
    pallas_call x1, Pallas kernels: 34.5 us -> 32.9 us  [per_device(): pl.pallas_call(kernel, out_shape=(jax.ShapeDtypeStruct((2, 8, 256), BF16)...]
where the time goes in v8:
time: 35.6 us; the launch traced here: 35.4 us
  Pallas kernels  34.8 us (98%)
  between operations  0.64 us (2%)
    pallas_call x1, Pallas kernels, per_device(): pl.pallas_call(kernel, out_shape=(jax.ShapeDtypeStruct((2, 8, 256), BF16)...  32.9 us
    pallas_call x1, Pallas kernels, per_device(): pl.pallas_call(hand_over, out_shape=(jax.ShapeDtypeStruct((2, 8, 256), BF...  1.87 us

profile of v8, /device:TPU:1, one launch (start us, length us, event | category | flops | bytes accessed | tf_op | source)
XLA Modules:
  0.0 35.4 jit_solution(1606430852791358965)
XLA Ops:
  0.6 32.9 %shard_map.95 = (bf16[2,8,256]{2,1,0:T(8,128)(2,1)}, bf16[4,2048]{1,0:T(4,128)(2,1)}) custom-call(bf16[32,128,2048]{2,1,0:T(8,128)(2,1)} %kv.1, bf16[2,8,256]{2,1,0:T(8,128)(2,1)} %q_in.1, bf16[2,8,64]{2,1,0:T(8,128)(2,1)} %nk_in.1, s32[32,128]{1,0:T(8,128)} %dev_in.1, s32[32,128]{1,0:T(8,128)} %slot_in.1, s32[2,32]{1,0:T(2,128)} %own_dev_in.1, ...), custom_call_target="tpu_custom_call" | custom-call | tf_op jit(solution)/shard_map/pallas_call | solution.py:606
  33.6 1.9 %shard_map.96 = (bf16[2,8,256]{2,1,0:T(8,128)(2,1)}, bf16[4,2048]{1,0:T(4,128)(2,1)}) custom-call(bf16[2,8,256]{2,1,0:T(8,128)(2,1)} %get-tuple-element.4.result, bf16[4,2048]{1,0:T(4,128)(2,1)} %get-tuple-element.5.rows), custom_call_target="tpu_custom_call" | custom-call | tf_op jit(solution)/shard_map/pallas_call | solution.py:671

commit v9 on v8

--- a/solution.py
+++ b/solution.py
@@ -43,7 +43,7 @@
 def kernel(
     kv, q_in, nk_in, dev_in, slot_in, own_dev_in, own_row_in, lens_in, out_at, tail_at,
     q, nk, dev, slot, own_dev, own_row, lens, out, tail,
-    info, kvb, gat, nx, tile, gnt, gq, gn, wb, pk, dn, cb, mx, mxr, mt, lift, uw, s32, r32, sb, rb, ss, rs, tl, meta, smeta, codes,
+    info, kvb, gat, nx, tile, gnt, gq, gn, wb, pk, dn, cb, cb2, mx, mxr, mt, lift, uw, s32, r32, sb, rb, ss, rs, tl, meta, smeta, codes,
     k_sem, v_sem, sg, rg, s_sib, r_sib, n_sems, s_m, r_m, s_chunk, r_chunk, b_sems, e_sems, meta_sem, io_sem,
 ):
     z = lax.axis_index("inst")
@@ -213,10 +213,13 @@
     rows, lanes = iota((SLOTS, 128), 0), iota((SLOTS, 128), 1)
     req_row = jnp.sum(jnp.where(rows == lanes, req_col, 0), axis=0, keepdims=True)
     req_row = jnp.where(lanes < SLOTS, jnp.broadcast_to(req_row, (SLOTS, 128)), -2)
-    before = jnp.max(jnp.where((req_row == req_col) & (lanes < rows), lanes, -1), axis=1, keepdims=True)
-    last = jnp.max(jnp.where(req_row == rows, lanes, -1), axis=1, keepdims=True)
+    same_half = (lanes >> 4) == (rows >> 4)
+    before = jnp.where((req_row == req_col) & (lanes < rows) & same_half, lanes, -1)
+    before = jnp.max(before, axis=1, keepdims=True)
+    low = jnp.max(jnp.where((req_row == rows) & (lanes < 16), lanes, -1), axis=1, keepdims=True)
+    high = jnp.max(jnp.where((req_row == rows) & (lanes >= 16), lanes - 16, -1), axis=1, keepdims=True)
     meta[:SLOTS] = jnp.where(
-        lanes == 0, req_col, jnp.where(lanes == 1, held, jnp.where(lanes == 2, before, last))
+        lanes == 0, req_col, jnp.where(lanes == 1, held, jnp.where(lanes == 2, before, jnp.where(lanes == 3, low, high)))
     )
     meta[SLOTS:] = found[SLOTS:]
     meta_copy = pltpu.make_async_copy(meta, smeta, meta_sem)
@@ -250,7 +253,7 @@
 
     @pl.loop(0, SLOTS)
     def _(n):
-        req, held, prev, end = smeta[n, 0], smeta[n, 1], smeta[n, 2], smeta[n, 3]
+        req, held, prev, low, high = [smeta[n, w] for w in range(5)]
         r = jnp.maximum(req, 0)
         b = (jnp.maximum(held, 1) - 1) & 127
         info[0, n] = req
@@ -258,9 +261,11 @@
         info[2, n] = r & 7
         info[3, n] = jnp.where(held > 0, lens[r] - b * 128, 0)
         info[4, n] = prev
-        info[5, n] = jnp.maximum(prev, 0)
-        info[6, n] = end
-        info[7, n] = jnp.maximum(end, 0)
+        info[5, n] = jnp.maximum(prev, 0) & 15
+        info[6, n] = low
+        info[7, n] = jnp.maximum(low, 0)
+        info[8, n] = high
+        info[9, n] = jnp.maximum(high, 0)
 
 
     @pl.loop(0, KV_PARTS)
@@ -334,15 +339,15 @@
 
         @pl.loop(0, SLOTS // GROUP, init_carry=jnp.zeros((32, 128), F32))
         def den(group, den):
-            for e in range(GROUP):
+            for e in [v for half in zip(range(16), range(16, 32)) for v in half]:
                 n = group * GROUP + e
                 r = info[0, n]
                 best = jnp.max(jnp.where(lanes == r, most, LOW), axis=1, keepdims=True)
                 factor = jnp.exp(pk[n] - best)
                 both = jnp.dot(wb[n], kvb[n, :, cols], preferred_element_type=F32)
                 num = jnp.concatenate([both[:16, :128], both[16:, 128:]], axis=0)
-                earlier = jnp.where(info[4, n] >= 0, cb[info[5, n]], 0.0)
-                cb[n] = num * factor + earlier
+                into, at = (cb, e) if e < 16 else (cb2, e - 16)
+                into[at] = num * factor + jnp.where(info[4, n] >= 0, into[info[5, n]], 0.0)
                 den = den + jnp.where(lanes == r, factor * dn[n], 0.0)
             return den
 
@@ -353,7 +358,10 @@
     def hand_on(k):
         for i in range(4):
             for rl in range(8):
-                sums = jnp.where(info[6, i * 8 + rl] >= 0, cb[info[7, i * 8 + rl]], 0.0)
+                r = i * 8 + rl
+                sums = jnp.where(info[6, r] >= 0, cb[info[7, r]], 0.0) + jnp.where(
+                    info[8, r] >= 0, cb2[info[9, r]], 0.0
+                )
                 for xh in range(2):
                     for of in range(2):
                         at = pl.ds(xh * 64 + rl, 8, stride=8)
@@ -447,21 +455,19 @@
                     for j in range(4):
                         gq[of, i, j * 32 : j * 32 + 32, :] = gat[of, kt, i * 4 + j].astype(F32)
 
-            most = scores(k)
-
-            @pl.when(k == 0)
-            def _():
-                arrived(1, ys[2], 15).wait_recv()
-                sib_copy(1, core).start()
-
             @pl.when(k == 1)
             def _():
                 for phase in (2, 3):
                     arrived(phase, ys[SHIFT[phase]], 16).wait_recv()
                     sib_copy(phase, core).start()
 
+            most = scores(k)
+
             @pl.when(k == 0)
             def _():
+                arrived(1, ys[2], 15).wait_recv()
+                sib_copy(1, core).start()
+
                 @pl.loop(0, KV_PARTS)
                 def _(part):
                     value_copy(part).wait()
@@ -589,14 +595,16 @@
         store.wait()
 
 
-def hand_over(result, rows, out, tail, sems):
-    copies = [
-        pltpu.make_async_copy(result, out, sems.at[0]),
-        pltpu.make_async_copy(rows, tail, sems.at[1]),
-    ]
-    for copy in copies:
+def hand_over(result, rows, out, tail, out_near, tail_near, sems):
+    ways = [(result, out_near, out), (rows, tail_near, tail)]
+    arrive = [pltpu.make_async_copy(a, b, sems.at[k]) for k, (a, b, _) in enumerate(ways)]
+    leave = [pltpu.make_async_copy(b, c, sems.at[k]) for k, (_, b, c) in enumerate(ways)]
+    for copy in arrive:
         copy.start()
-    for copy in copies:
+    for first, second in zip(arrive, leave):
+        first.wait()
+        second.start()
+    for copy in leave:
         copy.wait()
 
 
@@ -621,7 +629,7 @@
             pltpu.SMEM((REQS,), I32),
             pltpu.VMEM((2, 8, 256), BF16),
             pltpu.VMEM((4, 2048), BF16),
-            pltpu.SMEM((8, SLOTS), I32),
+            pltpu.SMEM((10, SLOTS), I32),
             pltpu.VMEM((SLOTS, 128, 2048), BF16),
             pltpu.VMEM((2, 4, 16, 32, 128), BF16),
             pltpu.VMEM((2, 8, 128), F32),
@@ -632,7 +640,8 @@
             pltpu.VMEM((SLOTS, 32, 128), BF16),
             pltpu.VMEM((SLOTS, 32, 128), F32),
             pltpu.VMEM((SLOTS, 32, 128), F32),
-            pltpu.VMEM((SLOTS, 32, 128), F32),
+            pltpu.VMEM((16, 32, 128), F32),
+            pltpu.VMEM((16, 32, 128), F32),
             pltpu.VMEM((4, 2, 32, 128), F32),
             pltpu.VMEM((4, 2, 32, 128), F32),
             pltpu.VMEM((64, 128), F32),
@@ -676,7 +685,7 @@
         ),
         in_specs=[anywhere] * 2,
         out_specs=(anywhere, anywhere),
-        scratch_shapes=[dma((2,))],
+        scratch_shapes=[pltpu.VMEM((2, 8, 256), BF16), pltpu.VMEM((4, 2048), BF16), dma((2,))],
     )(result, tail)
 
 

time: 35.6 us -> 35.6 us (level)
    pallas_call x1, Pallas kernels: 1.87 us -> 1.36 us  [per_device(): pl.pallas_call(hand_over, out_shape=(jax.ShapeDtypeStruct((2, 8, 256), BF...]
where the time goes in v9:
time: 35.6 us; the launch traced here: 35.2 us
  Pallas kernels  34.6 us (97%)
  between operations  0.64 us (2%)
    pallas_call x1, Pallas kernels, per_device(): pl.pallas_call(kernel, out_shape=(jax.ShapeDtypeStruct((2, 8, 256), BF16)...  33.2 us
    pallas_call x1, Pallas kernels, per_device(): pl.pallas_call(hand_over, out_shape=(jax.ShapeDtypeStruct((2, 8, 256), BF...  1.36 us

profile of v9, /device:TPU:1, one launch (start us, length us, event | category | flops | bytes accessed | tf_op | source)
XLA Modules:
  0.0 35.2 jit_solution(12570905622231591039)
XLA Ops:
  0.6 33.2 %shard_map.95 = (bf16[2,8,256]{2,1,0:T(8,128)(2,1)}, bf16[4,2048]{1,0:T(4,128)(2,1)}) custom-call(bf16[32,128,2048]{2,1,0:T(8,128)(2,1)} %kv.1, bf16[2,8,256]{2,1,0:T(8,128)(2,1)} %q_in.1, bf16[2,8,64]{2,1,0:T(8,128)(2,1)} %nk_in.1, s32[32,128]{1,0:T(8,128)} %dev_in.1, s32[32,128]{1,0:T(8,128)} %slot_in.1, s32[2,32]{1,0:T(2,128)} %own_dev_in.1, ...), custom_call_target="tpu_custom_call" | custom-call | tf_op jit(solution)/shard_map/pallas_call | solution.py:614
  33.8 1.4 %shard_map.96 = (bf16[2,8,256]{2,1,0:T(8,128)(2,1)}, bf16[4,2048]{1,0:T(4,128)(2,1)}) custom-call(bf16[2,8,256]{2,1,0:T(8,128)(2,1)} %get-tuple-element.4.result, bf16[4,2048]{1,0:T(4,128)(2,1)} %get-tuple-element.5.rows), custom_call_target="tpu_custom_call" | custom-call | tf_op jit(solution)/shard_map/pallas_call | solution.py:680

commit v10 on v8

--- a/solution.py
+++ b/solution.py
@@ -20,7 +20,7 @@
 SCALE = 1.0 / math.sqrt(128)
 UNROLL = 4
 GROUP = 32
-SHIFT = (0, 2, 1, 3)
+SHIFT = (0, 2, 3, 1)
 PLACES = (10, 9, 11, 6, 14, 2, 8, 5, 7, 13, 15, 1, 3, 4, 12)
 KV_PARTS = SLOTS // UNROLL
 
@@ -103,7 +103,7 @@
     pl.semaphore_wait(barrier, 19)
 
     def turn(k):
-        return (y + ((k & 1) << 1) + (k >> 1)) & 3
+        return (y + 2 * (k & 1) + 3 * (k >> 1)) & 3
 
     def push(block, k, to):
         return pltpu.make_async_remote_copy(
@@ -121,7 +121,7 @@
         return push(gat.at[core, ys[2], spot], 1, place(*beside(e, y)))
 
     def next_copy(m):
-        return push(gat.at[core, y], 2 if m == 3 else 3, place(z, ys[m], x))
+        return push(gat.at[core, y], 3 if m == 3 else 2, place(z, ys[m], x))
 
     def arrived(k, plane, blocks):
         return push(gat.at[core, plane, pl.ds(0, blocks)], k, sibling)
@@ -237,7 +237,7 @@
 
     arrived(0, y, 15).wait_recv()
     sib_copy(0, core).start()
-    for m in (3, 1):
+    for m in (1, 3):
         next_copy(m).start()
 
     for of in range(2):
@@ -567,7 +567,7 @@
     across_copy().wait_send()
     arrived(0, y, 15).wait_send()
     arrived(1, y, 15).wait_send()
-    for m in (3, 1):
+    for m in (1, 3):
         next_copy(m).wait_send()
     for k in range(4):
         sib_copy(k, core).wait_send()
@@ -589,14 +589,16 @@
         store.wait()
 
 
-def hand_over(result, rows, out, tail, sems):
-    copies = [
-        pltpu.make_async_copy(result, out, sems.at[0]),
-        pltpu.make_async_copy(rows, tail, sems.at[1]),
-    ]
-    for copy in copies:
+def hand_over(result, rows, out, tail, out_near, tail_near, sems):
+    ways = [(result, out_near, out), (rows, tail_near, tail)]
+    arrive = [pltpu.make_async_copy(a, b, sems.at[k]) for k, (a, b, _) in enumerate(ways)]
+    leave = [pltpu.make_async_copy(b, c, sems.at[k]) for k, (_, b, c) in enumerate(ways)]
+    for copy in arrive:
         copy.start()
-    for copy in copies:
+    for first, second in zip(arrive, leave):
+        first.wait()
+        second.start()
+    for copy in leave:
         copy.wait()
 
 
@@ -676,7 +678,7 @@
         ),
         in_specs=[anywhere] * 2,
         out_specs=(anywhere, anywhere),
-        scratch_shapes=[dma((2,))],
+        scratch_shapes=[pltpu.VMEM((2, 8, 256), BF16), pltpu.VMEM((4, 2048), BF16), dma((2,))],
     )(result, tail)
 
 

time: 35.6 us -> 35.8 us (level)
    pallas_call x1, Pallas kernels: 32.9 us -> 33.6 us  [per_device(): pl.pallas_call(kernel, out_shape=(jax.ShapeDtypeStruct((2, 8, 256), BF16)...]
    pallas_call x1, Pallas kernels: 1.87 us -> 1.36 us  [per_device(): pl.pallas_call(hand_over, out_shape=(jax.ShapeDtypeStruct((2, 8, 256), BF...]
where the time goes in v10:
time: 35.8 us; the launch traced here: 35.6 us
  Pallas kernels  34.9 us (97%)
  between operations  0.64 us (2%)
    pallas_call x1, Pallas kernels, per_device(): pl.pallas_call(kernel, out_shape=(jax.ShapeDtypeStruct((2, 8, 256), BF16)...  33.6 us
    pallas_call x1, Pallas kernels, per_device(): pl.pallas_call(hand_over, out_shape=(jax.ShapeDtypeStruct((2, 8, 256), BF...  1.36 us

profile of v10, /device:TPU:1, one launch (start us, length us, event | category | flops | bytes accessed | tf_op | source)
XLA Modules:
  0.0 35.6 jit_solution(2723011476987150922)
XLA Ops:
  0.6 33.6 %shard_map.95 = (bf16[2,8,256]{2,1,0:T(8,128)(2,1)}, bf16[4,2048]{1,0:T(4,128)(2,1)}) custom-call(bf16[32,128,2048]{2,1,0:T(8,128)(2,1)} %kv.1, bf16[2,8,256]{2,1,0:T(8,128)(2,1)} %q_in.1, bf16[2,8,64]{2,1,0:T(8,128)(2,1)} %nk_in.1, s32[32,128]{1,0:T(8,128)} %dev_in.1, s32[32,128]{1,0:T(8,128)} %slot_in.1, s32[2,32]{1,0:T(2,128)} %own_dev_in.1, ...), custom_call_target="tpu_custom_call" | custom-call | tf_op jit(solution)/shard_map/pallas_call | solution.py:608
  34.2 1.4 %shard_map.96 = (bf16[2,8,256]{2,1,0:T(8,128)(2,1)}, bf16[4,2048]{1,0:T(4,128)(2,1)}) custom-call(bf16[2,8,256]{2,1,0:T(8,128)(2,1)} %get-tuple-element.4.result, bf16[4,2048]{1,0:T(4,128)(2,1)} %get-tuple-element.5.rows), custom_call_target="tpu_custom_call" | custom-call | tf_op jit(solution)/shard_map/pallas_call | solution.py:673

commit v11 on v10

--- a/solution.py
+++ b/solution.py
@@ -20,7 +20,7 @@
 SCALE = 1.0 / math.sqrt(128)
 UNROLL = 4
 GROUP = 32
-SHIFT = (0, 2, 3, 1)
+SHIFT = (0, 2, 1, 3)
 PLACES = (10, 9, 11, 6, 14, 2, 8, 5, 7, 13, 15, 1, 3, 4, 12)
 KV_PARTS = SLOTS // UNROLL
 
@@ -103,7 +103,7 @@
     pl.semaphore_wait(barrier, 19)
 
     def turn(k):
-        return (y + 2 * (k & 1) + 3 * (k >> 1)) & 3
+        return (y + ((k & 1) << 1) + (k >> 1)) & 3
 
     def push(block, k, to):
         return pltpu.make_async_remote_copy(
@@ -121,7 +121,7 @@
         return push(gat.at[core, ys[2], spot], 1, place(*beside(e, y)))
 
     def next_copy(m):
-        return push(gat.at[core, y], 3 if m == 3 else 2, place(z, ys[m], x))
+        return push(gat.at[core, y], 2 if m == 3 else 3, place(z, ys[m], x))
 
     def arrived(k, plane, blocks):
         return push(gat.at[core, plane, pl.ds(0, blocks)], k, sibling)
@@ -237,7 +237,7 @@
 
     arrived(0, y, 15).wait_recv()
     sib_copy(0, core).start()
-    for m in (1, 3):
+    for m in (3, 1):
         next_copy(m).start()
 
     for of in range(2):
@@ -567,7 +567,7 @@
     across_copy().wait_send()
     arrived(0, y, 15).wait_send()
     arrived(1, y, 15).wait_send()
-    for m in (1, 3):
+    for m in (3, 1):
         next_copy(m).wait_send()
     for k in range(4):
         sib_copy(k, core).wait_send()

time: 35.8 us -> 35.1 us (0.980)
  Pallas kernels: 34.9 us -> 34.3 us
    pallas_call x1, Pallas kernels: 33.6 us -> 32.9 us  [per_device(): pl.pallas_call(kernel, out_shape=(jax.ShapeDtypeStruct((2, 8, 256), BF16)...]
where the time goes in v11:
time: 35.1 us; the launch traced here: 34.9 us
  Pallas kernels  34.3 us (98%)
  between operations  0.64 us (2%)
    pallas_call x1, Pallas kernels, per_device(): pl.pallas_call(kernel, out_shape=(jax.ShapeDtypeStruct((2, 8, 256), BF16)...  32.9 us
    pallas_call x1, Pallas kernels, per_device(): pl.pallas_call(hand_over, out_shape=(jax.ShapeDtypeStruct((2, 8, 256), BF...  1.36 us

profile of v11, /device:TPU:1, one launch (start us, length us, event | category | flops | bytes accessed | tf_op | source)
XLA Modules:
  0.0 34.9 jit_solution(15880451989300718609)
XLA Ops:
  0.6 32.9 %shard_map.95 = (bf16[2,8,256]{2,1,0:T(8,128)(2,1)}, bf16[4,2048]{1,0:T(4,128)(2,1)}) custom-call(bf16[32,128,2048]{2,1,0:T(8,128)(2,1)} %kv.1, bf16[2,8,256]{2,1,0:T(8,128)(2,1)} %q_in.1, bf16[2,8,64]{2,1,0:T(8,128)(2,1)} %nk_in.1, s32[32,128]{1,0:T(8,128)} %dev_in.1, s32[32,128]{1,0:T(8,128)} %slot_in.1, s32[2,32]{1,0:T(2,128)} %own_dev_in.1, ...), custom_call_target="tpu_custom_call" | custom-call | tf_op jit(solution)/shard_map/pallas_call | solution.py:608
  33.6 1.4 %shard_map.96 = (bf16[2,8,256]{2,1,0:T(8,128)(2,1)}, bf16[4,2048]{1,0:T(4,128)(2,1)}) custom-call(bf16[2,8,256]{2,1,0:T(8,128)(2,1)} %get-tuple-element.4.result, bf16[4,2048]{1,0:T(4,128)(2,1)} %get-tuple-element.5.rows), custom_call_target="tpu_custom_call" | custom-call | tf_op jit(solution)/shard_map/pallas_call | solution.py:673

commit v12 on v11

--- a/solution.py
+++ b/solution.py
@@ -439,14 +439,16 @@
     def _(k):
         @pl.when(k < 4)
         def _():
-            sib_copy(k, sib).wait_recv()
-
             kt = turn(k)
-            for of in range(2):
+
+            def widen(of):
                 for i in range(4):
                     for j in range(4):
                         gq[of, i, j * 32 : j * 32 + 32, :] = gat[of, kt, i * 4 + j].astype(F32)
 
+            widen(core)
+            sib_copy(k, sib).wait_recv()
+            widen(sib)
             most = scores(k)
 
             @pl.when(k == 0)

time: 35.1 us -> 35.2 us (level)
  no operation moved by 1% of the time
where the time goes in v12:
time: 35.2 us; the launch traced here: 35 us
  Pallas kernels  34.3 us (97%)
  between operations  0.64 us (2%)
    pallas_call x1, Pallas kernels, per_device(): pl.pallas_call(kernel, out_shape=(jax.ShapeDtypeStruct((2, 8, 256), BF16)...  33 us
    pallas_call x1, Pallas kernels, per_device(): pl.pallas_call(hand_over, out_shape=(jax.ShapeDtypeStruct((2, 8, 256), BF...  1.36 us

profile of v12, /device:TPU:1, one launch (start us, length us, event | category | flops | bytes accessed | tf_op | source)
XLA Modules:
  0.0 35.0 jit_solution(4162154417211691476)
XLA Ops:
  0.6 33.0 %shard_map.95 = (bf16[2,8,256]{2,1,0:T(8,128)(2,1)}, bf16[4,2048]{1,0:T(4,128)(2,1)}) custom-call(bf16[32,128,2048]{2,1,0:T(8,128)(2,1)} %kv.1, bf16[2,8,256]{2,1,0:T(8,128)(2,1)} %q_in.1, bf16[2,8,64]{2,1,0:T(8,128)(2,1)} %nk_in.1, s32[32,128]{1,0:T(8,128)} %dev_in.1, s32[32,128]{1,0:T(8,128)} %slot_in.1, s32[2,32]{1,0:T(2,128)} %own_dev_in.1, ...), custom_call_target="tpu_custom_call" | custom-call | tf_op jit(solution)/shard_map/pallas_call | solution.py:610
  33.6 1.4 %shard_map.96 = (bf16[2,8,256]{2,1,0:T(8,128)(2,1)}, bf16[4,2048]{1,0:T(4,128)(2,1)}) custom-call(bf16[2,8,256]{2,1,0:T(8,128)(2,1)} %get-tuple-element.4.result, bf16[4,2048]{1,0:T(4,128)(2,1)} %get-tuple-element.5.rows), custom_call_target="tpu_custom_call" | custom-call | tf_op jit(solution)/shard_map/pallas_call | solution.py:675

commit v13 on v9

--- a/solution.py
+++ b/solution.py
@@ -455,19 +455,21 @@
                     for j in range(4):
                         gq[of, i, j * 32 : j * 32 + 32, :] = gat[of, kt, i * 4 + j].astype(F32)
 
+            most = scores(k)
+
+            @pl.when(k == 0)
+            def _():
+                arrived(1, ys[2], 15).wait_recv()
+                sib_copy(1, core).start()
+
             @pl.when(k == 1)
             def _():
                 for phase in (2, 3):
                     arrived(phase, ys[SHIFT[phase]], 16).wait_recv()
                     sib_copy(phase, core).start()
 
-            most = scores(k)
-
             @pl.when(k == 0)
             def _():
-                arrived(1, ys[2], 15).wait_recv()
-                sib_copy(1, core).start()
-
                 @pl.loop(0, KV_PARTS)
                 def _(part):
                     value_copy(part).wait()

time: 35.6 us -> 35.3 us (level)
  no operation moved by 1% of the time
where the time goes in v13:
time: 35.3 us; the launch traced here: 35.1 us
  Pallas kernels  34.5 us (98%)
  between operations  0.64 us (2%)
    pallas_call x1, Pallas kernels, per_device(): pl.pallas_call(kernel, out_shape=(jax.ShapeDtypeStruct((2, 8, 256), BF16)...  33.1 us
    pallas_call x1, Pallas kernels, per_device(): pl.pallas_call(hand_over, out_shape=(jax.ShapeDtypeStruct((2, 8, 256), BF...  1.36 us

profile of v13, /device:TPU:1, one launch (start us, length us, event | category | flops | bytes accessed | tf_op | source)
XLA Modules:
  0.0 35.1 jit_solution(11852529604990900191)
XLA Ops:
  0.6 33.1 %shard_map.95 = (bf16[2,8,256]{2,1,0:T(8,128)(2,1)}, bf16[4,2048]{1,0:T(4,128)(2,1)}) custom-call(bf16[32,128,2048]{2,1,0:T(8,128)(2,1)} %kv.1, bf16[2,8,256]{2,1,0:T(8,128)(2,1)} %q_in.1, bf16[2,8,64]{2,1,0:T(8,128)(2,1)} %nk_in.1, s32[32,128]{1,0:T(8,128)} %dev_in.1, s32[32,128]{1,0:T(8,128)} %slot_in.1, s32[2,32]{1,0:T(2,128)} %own_dev_in.1, ...), custom_call_target="tpu_custom_call" | custom-call | tf_op jit(solution)/shard_map/pallas_call | solution.py:616
  33.8 1.4 %shard_map.96 = (bf16[2,8,256]{2,1,0:T(8,128)(2,1)}, bf16[4,2048]{1,0:T(4,128)(2,1)}) custom-call(bf16[2,8,256]{2,1,0:T(8,128)(2,1)} %get-tuple-element.4.result, bf16[4,2048]{1,0:T(4,128)(2,1)} %get-tuple-element.5.rows), custom_call_target="tpu_custom_call" | custom-call | tf_op jit(solution)/shard_map/pallas_call | solution.py:682
